TPU v7x, 512 devices: a whole 4x4x16 slice. The times are simulated.
512 devices in a mesh: section: 16 (over x, y), expert: 32 (over z, core).
Axes of the slice: x: 4, y: 4, z: 16, core: 2. Of those that a mesh axis runs over, the one named last changes fastest.
Arguments:
- activations: bfloat16 [16, 4096, 2048], P('section', 'expert'), may hold values from -60 to 60
- cotangents: bfloat16 [16, 4096, 2048], P('section', 'expert'), may hold values from -6 to 6
- norm_gain: bfloat16 [16, 2048], P('section'), may hold values from 0.25 to 1.75
- routes: int32 [16, 4096, 2], P('section', 'expert'), may hold values from 0 to 15, all different within a row; in each aligned block of 128 rows (0 to 127, 128 to 255, ..., all dimensions but the last counted through in order) at most 24 rows name the same one
- lengths: int32 [16, 32], P('section', 'expert'), may hold values from 64 to 128, as said below
- router_weight: bfloat16 [16, 2048, 16], P('section'), may hold values from -0.125 to 0.125
- gate_weight: bfloat16 [16, 32, 2048, 256], P('section', 'expert'), may hold values from -0.125 to 0.125
- up_weight: bfloat16 [16, 32, 2048, 256], P('section', 'expert'), may hold values from -0.125 to 0.125
- down_weight: bfloat16 [16, 32, 256, 2048], P('section', 'expert'), may hold values from -0.25 to 0.25
Outputs:
- layer_input_gradient: bfloat16 [16, 4096, 2048], P('section', 'expert')
- router_grad: float32 [16, 2048, 16], P('section')
- norm_gain_gradient: float32 [16, 2048], P('section')
Inputs may be any that keep to these rules, and one draw needn't show every extreme that they name: `routes`: each row names 2 different experts; among the rows of one device, padding rows included, no expert is named more than 24 times, a bound that some block reaches there in every draw. The first lengths[s, b] rows of each device's block are live, the rest are padding; some device's block is full in every draw.
All inputs are finite; a program needn't handle non-finite values.
Results may differ from a plain program's by a relative error of at most 0.03.
Values may be sent and summed in bfloat16 or wider, within the bound.
A program may use at most 128 MiB of HBM per device.

v0:
```python
import jax
import jax.numpy as jnp
from jax import lax
from jax.sharding import PartitionSpec as P

EPSILON = 1e-05


def from_behind(value, axis, steps):
    count = lax.axis_size(axis)
    pairs = [(source, (source + steps) % count) for source in range(count)]
    return lax.ppermute(value, axis, pairs)


def expert_forward(rows_in, gate_half, up_half, down_half):
    gate_pre = jnp.dot(rows_in, gate_half, preferred_element_type=jnp.float32)
    up_pre = jnp.dot(rows_in, up_half, preferred_element_type=jnp.float32)
    logistic = jax.nn.sigmoid(gate_pre)
    hidden = (gate_pre * logistic * up_pre).astype(jnp.bfloat16)
    expert_out = jnp.dot(hidden, down_half, preferred_element_type=jnp.float32).astype(jnp.bfloat16)
    return (gate_pre, up_pre, logistic, expert_out)


def expert_backward(grad_rows, gate_pre, up_pre, logistic, gate_half, up_half, down_half):
    contract = (((1,), (1,)), ((), ()))
    hidden_grad = lax.dot_general(
        grad_rows, down_half, contract, preferred_element_type=jnp.float32
    )
    gate_grad = (hidden_grad * up_pre * logistic * (1.0 + gate_pre * (1.0 - logistic))).astype(
        jnp.bfloat16
    )
    up_grad = (hidden_grad * gate_pre * logistic).astype(jnp.bfloat16)
    both_grads = jnp.concatenate([gate_grad, up_grad], axis=1)
    both_weights = jnp.concatenate([gate_half, up_half], axis=1)
    total = lax.dot_general(both_grads, both_weights, contract, preferred_element_type=jnp.float32)
    return total.astype(jnp.bfloat16)


def deliver(stacked, device_count, capacity, model_width):
    stack_count = stacked.shape[0]
    expert_count = stacked.shape[1] // capacity
    shaped = stacked.reshape(stack_count, expert_count, 1, capacity * model_width)
    doubled = jnp.broadcast_to(shaped, (stack_count, expert_count, 2, capacity * model_width))
    doubled = doubled.reshape(stack_count, device_count * capacity, model_width)
    return lax.all_to_all(doubled, "expert", split_axis=1, concat_axis=1, tiled=True)


def send_outputs(expert_out):
    return lax.all_to_all(expert_out, "expert", split_axis=0, concat_axis=0, tiled=True)


def send_backs(expert_back):
    return lax.all_to_all(expert_back, "expert", split_axis=0, concat_axis=0, tiled=True)


def halves_total(received, expert_count, capacity, model_width):
    view = received.reshape(expert_count, 2 * capacity, model_width)
    total = view[:, :capacity].astype(jnp.float32) + view[:, capacity:].astype(jnp.float32)
    return total.reshape(expert_count * capacity, model_width)


def per_device(
    activations,
    cotangents,
    norm_gain,
    routes,
    lengths,
    router_weight,
    gate_weight,
    up_weight,
    down_weight,
):
    arriving = from_behind(activations, "section", 1)[0]
    returned_cotangents = from_behind(cotangents, "section", -1)[0]
    row_count = arriving.shape[0]
    model_width = arriving.shape[1]
    expert_count = router_weight.shape[2]
    top_count = routes.shape[2]
    device_count = lax.axis_size("expert")
    capacity = 3 * row_count * top_count // (2 * expert_count)
    complete_input = arriving.astype(jnp.float32)
    mean_sq = jnp.mean(complete_input * complete_input, axis=-1, keepdims=True)
    inverse_root_mean = lax.rsqrt(mean_sq + EPSILON)
    unit_input = complete_input * inverse_root_mean
    gain_broadcast = norm_gain[0].astype(jnp.float32)
    normalized_rows = (unit_input * gain_broadcast).astype(jnp.bfloat16)
    router = router_weight[0]
    logits = jnp.dot(normalized_rows, router, preferred_element_type=jnp.float32)
    picks = routes[0]
    expert_ids = jnp.arange(expert_count, dtype=jnp.int32)
    onehot = (picks[:, :, None] == expert_ids[None, None, :]).astype(jnp.float32)
    chosen = jnp.sum(onehot * logits[:, None, :], axis=2)
    gates = 1.0 / jnp.sum(jnp.exp(chosen[:, None, :] - chosen[:, :, None]), axis=2)
    live = jnp.arange(row_count, dtype=jnp.int32) < lengths[0, 0]
    flat_picks = picks.reshape(-1)
    pair_live = jnp.repeat(live, top_count)
    hot = ((flat_picks[:, None] == expert_ids[None, :]) & pair_live[:, None]).astype(jnp.int32)
    place_index = jnp.sum((jnp.cumsum(hot, axis=0) - hot) * hot, axis=1)
    target = jnp.where(pair_live, flat_picks * capacity + place_index, -1)
    slot_ids = jnp.arange(expert_count * capacity, dtype=jnp.int32)
    select = (target[:, None] == slot_ids[None, :]).astype(jnp.bfloat16)
    scatter_rows = jnp.sum(select.reshape(row_count, top_count, -1), axis=1)
    by_rows = (((0,), (0,)), ((), ()))
    row_buffer = lax.dot_general(
        scatter_rows, normalized_rows, by_rows, preferred_element_type=jnp.float32
    ).astype(jnp.bfloat16)
    grad_buffer = lax.dot_general(
        scatter_rows, returned_cotangents, by_rows, preferred_element_type=jnp.float32
    ).astype(jnp.bfloat16)
    gate_half = gate_weight[0, 0]
    up_half = up_weight[0, 0]
    down_half = down_weight[0, 0]
    out_halves = None
    received_rows = deliver(row_buffer[None], device_count, capacity, model_width)
    gate_pre, up_pre, logistic, expert_out = expert_forward(
        received_rows[0], gate_half, up_half, down_half
    )
    out_halves = send_outputs(expert_out)
    received_grads = deliver(grad_buffer[None], device_count, capacity, model_width)
    grads_flat = received_grads[0]
    expert_back = expert_backward(
        grads_flat, gate_pre, up_pre, logistic, gate_half, up_half, down_half
    )
    back_halves = send_backs(expert_back)
    out_sum = halves_total(out_halves, expert_count, capacity, model_width)
    slot_score = jnp.sum(out_sum * grad_buffer.astype(jnp.float32), axis=-1)
    select_float = select.astype(jnp.float32)
    gate_share = jnp.dot(select_float, slot_score, precision=lax.Precision.HIGHEST).reshape(
        row_count, top_count
    )
    back_sum = halves_total(back_halves, expert_count, capacity, model_width)
    select_rows = select_float.reshape(row_count, top_count, -1)
    weighted = select_rows[:, 0, :] * gates[:, 0:1]
    weighted = weighted + select_rows[:, 1, :] * gates[:, 1:2]
    moe_grad = jnp.dot(weighted, back_sum, precision=lax.Precision.HIGHEST)
    select_grad = gates * (gate_share - jnp.sum(gates * gate_share, axis=-1, keepdims=True))
    logit_grad = jnp.einsum("rke,rk->re", onehot, select_grad)
    normalized_gradient = moe_grad + jnp.dot(
        logit_grad, router.astype(jnp.float32).T, precision=lax.Precision.HIGHEST
    )
    router_term = lax.dot_general(
        normalized_rows.astype(jnp.float32), logit_grad, by_rows, precision=lax.Precision.HIGHEST
    )
    gain_contribution = jnp.sum(normalized_gradient * unit_input, axis=0)
    router_total, gain_total = (
        lax.psum(router_term.astype(jnp.bfloat16), "expert").astype(jnp.float32),
        lax.psum(gain_contribution.astype(jnp.bfloat16), "expert").astype(jnp.float32),
    )
    gain_scaled_rows = normalized_gradient * gain_broadcast
    layer_input_gradient = returned_cotangents.astype(jnp.float32) + inverse_root_mean * (
        gain_scaled_rows
        - unit_input * jnp.mean(gain_scaled_rows * unit_input, axis=-1, keepdims=True)
    )
    return (layer_input_gradient.astype(jnp.bfloat16)[None], router_total[None], gain_total[None])


def solution(mesh):
    in_specs = (
        P("section", "expert", None),
        P("section", "expert", None),
        P("section", None),
        P("section", "expert", None),
        P("section", "expert"),
        P("section", None, None),
        P("section", "expert", None, None),
        P("section", "expert", None, None),
        P("section", "expert", None, None),
    )
    out_specs = (P("section", "expert", None), P("section", None, None), P("section", None))
    return jax.shard_map(
        per_device, mesh=mesh, in_specs=in_specs, out_specs=out_specs, check_vma=False
    )
```

profile of v0, /device:TPU:1, one launch (start us, length us, event | category | flops | bytes accessed | tf_op | source)
XLA Modules:
  0.0 910.5 jit_solution(16318494014032798691)
XLA Ops:
  7.2 7.8 collective-permute-start
  15.0 0.8 copy.32
  15.8 0.1 eq.54
  15.9 0.1 eq.58
  16.7 0.1 broadcast_in_dim.56
  16.8 0.1 and.16
  17.0 0.1 broadcast_in_dim.57
  17.1 0.1 broadcast_in_dim.58
  17.2 0.6 reduce-window.6
  17.8 0.2 slice_reduce_fusion
  18.0 0.1 fusion.60
  18.1 0.1 reduce_sum.88
  18.3 0.1 add_select_fusion
  18.4 0.1 fusion.45
  18.6 7.1 collective-permute-done
  25.7 0.6 convolution_convert_fusion.3
  26.3 1.7 broadcast_in_dim.60
  27.9 5.5 broadcast_in_dim.61
  33.5 11.5 %broadcast_in_dim.71 = bf16[1,768,2048]{2,0,1:T(2,128)(2,1)} reshape(bf16[16,2,49152]{2,1,0:T(2,128)(2,1)} %broadcast_in_dim.61) | data formatting | bytes 6291456 | tf_op jit(solution)/shard_map/broadcast_in_dim | solution.py:43
  44.9 0.5 broadcast.116
  45.4 20.6 %reduce.5 = bf16[768,2048]{1,0:T(8,128)(2,1)} reduce(bf16[768,1,2048]{2,1,0:T(2,128)(2,1)} %bitcast.129, bf16[]{:T(256)} %broadcast.116), dimensions={1}, to_apply=%bitcast.110.reduce_sub_computation | reduce | bytes 6291458
  66.0 8.4 reshape.165
  74.4 17.2 %all-to-all-start = ((bf16[32,2,24576]{2,1,0:T(2,128)(2,1)}), bf16[32,2,24576]{2,1,0:T(2,128)(2,1)}, u32[]{:S(2)}, u32[]{:S(2)}) async-start(bf16[32,2,24576]{2,1,0:T(2,128)(2,1)} %reshape.165), calls=%async_computation | async-start | bytes 6291456 | tf_op jit(solution)/shard_map/all_to_all | solution.py:45
  91.6 2.1 collective-permute-start.1
  93.7 17.6 %collective-permute-done.1 = bf16[1,128,2048]{2,1,0:T(8,128)(2,1)S(1)} collective-permute-done((bf16[1,128,2048]{2,1,0:T(8,128)(2,1)}, bf16[1,128,2048]{2,1,0:T(8,128)(2,1)S(1)}, u32[]{:S(2)}, u32[]{:S(2)}) %collective-permute-start.1) | collective-permute-done | bytes 524320 | tf_op jit(solution)/shard_map/ppermute | solution.py:12
  111.3 0.2 fusion.27
  111.5 1.9 convolution_convert_fusion.2
  113.4 2.7 broadcast_in_dim.63
  116.1 5.5 broadcast_in_dim.64
  121.7 11.5 %broadcast_in_dim.72 = bf16[1,768,2048]{2,0,1:T(2,128)(2,1)} reshape(bf16[16,2,49152]{2,1,0:T(2,128)(2,1)} %broadcast_in_dim.64) | data formatting | bytes 6291456 | tf_op jit(solution)/shard_map/broadcast_in_dim | solution.py:43
  133.1 20.6 %reduce.6 = bf16[768,2048]{1,0:T(8,128)(2,1)} reduce(bf16[768,1,2048]{2,1,0:T(2,128)(2,1)} %bitcast.130, bf16[]{:T(256)} %broadcast.116), dimensions={1}, to_apply=%bitcast.112.reduce_sub_computation | reduce | bytes 6291458
  153.7 8.4 reshape.167
  162.1 70.5 %all-to-all-done = bf16[32,2,24576]{2,1,0:T(2,128)(2,1)} async-done(((bf16[32,2,24576]{2,1,0:T(2,128)(2,1)}), bf16[32,2,24576]{2,1,0:T(2,128)(2,1)}, u32[]{:S(2)}, u32[]{:S(2)}) %all-to-all-start) | async-done | bytes 3145760 | tf_op jit(solution)/shard_map/all_to_all | solution.py:45
  232.6 7.8 all-to-all-start.1
  240.4 19.0 %reshape.166 = bf16[768,1,2048]{2,1,0:T(2,128)(2,1)} reshape(bf16[32,2,24576]{2,1,0:T(2,128)(2,1)} %all-to-all-done) | data formatting | bytes 6291456
  259.3 5.9 fusion.4
  265.2 116.6 %all-to-all-done.1 = bf16[32,2,24576]{2,1,0:T(2,128)(2,1)} async-done(((bf16[32,2,24576]{2,1,0:T(2,128)(2,1)}), bf16[32,2,24576]{2,1,0:T(2,128)(2,1)}, u32[]{:S(2)}, u32[]{:S(2)}) %all-to-all-start.1) | async-done | bytes 3145760 | tf_op jit(solution)/shard_map/all_to_all | solution.py:45
  381.8 18.9 %reshape.168 = bf16[768,1,2048]{2,1,0:T(2,128)(2,1)} reshape(bf16[32,2,24576]{2,1,0:T(2,128)(2,1)} %all-to-all-done.1) | data formatting | bytes 6291456
  400.8 5.4 fusion.2
  406.3 6.4 multiply_convert_fusion.2
  412.6 3.6 convolution_convert_fusion
  416.2 7.7 all-to-all-start.2
  423.9 4.1 convolution_convert_fusion.1
  428.0 136.9 %all-to-all-done.2 = bf16[32,24,2048]{2,1,0:T(8,128)(2,1)} async-done(((bf16[32,24,2048]{2,1,0:T(8,128)(2,1)}), bf16[32,24,2048]{2,1,0:T(8,128)(2,1)}, u32[]{:S(2)}, u32[]{:S(2)}) %all-to-all-start.2) | async-done | bytes 3145760 | tf_op jit(solution)/shard_map/all_to_all | solution.py:53
  565.0 7.7 all-to-all-start.3
  572.7 0.3 all-reduce.2.cloned.1.call-start
  573.0 0.1 copy.37
  573.1 0.1 fusion.46
  573.2 1.2 fusion.36
  574.4 0.6 exponential_reduce_fusion
  575.0 4.1 convert_add_fusion.1
  579.1 134.7 %all-to-all-done.3 = bf16[32,24,2048]{2,1,0:T(8,128)(2,1)} async-done(((bf16[32,24,2048]{2,1,0:T(8,128)(2,1)}), bf16[32,24,2048]{2,1,0:T(8,128)(2,1)}, u32[]{:S(2)}, u32[]{:S(2)}) %all-to-all-start.3) | async-done | bytes 3145760 | tf_op jit(solution)/shard_map/all_to_all | solution.py:49
  713.8 2.5 convert_add_fusion
  716.3 0.4 fusion.7
  716.8 0.3 fusion.43
  717.2 1.0 copy-done.1
  718.2 2.1 fusion.49
  720.3 1.0 fusion.26
  721.3 1.1 fusion.8
  722.4 1.2 fusion.38
  723.6 48.8 %psum.15 = bf16[1,2048]{1,0:T(2,128)(2,1)S(1)} all-reduce(bf16[1,2048]{1,0:T(2,128)(2,1)S(1)} %broadcast_in_dim.69), channel_id=1, replica_groups=mesh['section'=16,'expert'=32] {'expert'}, use_global_device_ids=true, to_apply=%region_12.13 | all-reduce | flops 2048 | bytes 8192 | tf_op jit(solution)/shard_map/psum | solution.py:147
  772.5 0.6 broadcast_in_dim.70
  773.1 129.1 %all-reduce.2.cloned.1.call-done = bf16[1,2048,16]{1,2,0:T(8,128)(2,1)} async-done(((bf16[1,2048,16]{1,2,0:T(8,128)(2,1)}), bf16[1,2048,16]{1,2,0:T(8,128)(2,1)}) %all-reduce.2.cloned.1.call-update) | async-done | bytes 65552 | tf_op jit(solution)/shard_map/psum | solution.py:146
  902.1 1.5 broadcast_in_dim.68
  (44 shorter events, 0.3 us)
Async XLA Ops:
  7.2 252.2 %copy-start = (bf16[1,1,256,2048]{3,2,1,0:T(8,128)(2,1)S(1)}, bf16[1,1,256,2048]{3,2,1,0:T(8,128)(2,1)}, u32[]{:S(2)}) copy-start(bf16[1,1,256,2048]{3,2,1,0:T(8,128)(2,1)} %param.17) | copy-start | bytes 3145732
  7.2 18.5 %collective-permute-start = (bf16[1,128,2048]{2,1,0:T(8,128)(2,1)}, bf16[1,128,2048]{2,1,0:T(8,128)(2,1)S(1)}, u32[]{:S(2)}, u32[]{:S(2)}) collective-permute-start(bf16[1,128,2048]{2,1,0:T(8,128)(2,1)} %param.10), channel_id=1, source_target_pairs={{0,480},{32,0},{64,32},{96,64},{128,96},{160,128},{192,160},{224,1... | collective-permute-start | bytes 1572872 | tf_op jit(solution)/shard_map/ppermute | solution.py:12
  25.7 7.8 copy-start.2
  74.4 19.3 %copy-start.5 = (bf16[1,2048]{1,0:T(2,128)(2,1)S(1)}, bf16[1,2048]{1,0:T(2,128)(2,1)}, u32[]{:S(2)}) copy-start(bf16[1,2048]{1,0:T(2,128)(2,1)} %param.11) | copy-start | bytes 12292
  74.4 158.2 %all-to-all-start = ((bf16[32,2,24576]{2,1,0:T(2,128)(2,1)}), bf16[32,2,24576]{2,1,0:T(2,128)(2,1)}, u32[]{:S(2)}, u32[]{:S(2)}) async-start(bf16[32,2,24576]{2,1,0:T(2,128)(2,1)} %reshape.165), calls=%async_computation | async-start | bytes 6291456 | tf_op jit(solution)/shard_map/all_to_all | solution.py:45
  91.6 19.7 %collective-permute-start.1 = (bf16[1,128,2048]{2,1,0:T(8,128)(2,1)}, bf16[1,128,2048]{2,1,0:T(8,128)(2,1)S(1)}, u32[]{:S(2)}, u32[]{:S(2)}) collective-permute-start(bf16[1,128,2048]{2,1,0:T(8,128)(2,1)} %param.9), channel_id=1, source_target_pairs={{0,32},{32,64},{64,96},{96,128},{128,160},{160,192},{192,224},{224... | collective-permute-start | bytes 1572872 | tf_op jit(solution)/shard_map/ppermute | solution.py:12
  111.5 10.2 %copy-start.6 = (f32[128]{0:T(128)}, f32[128]{0:T(128)S(1)}, u32[]{:S(2)}) copy-start(f32[128]{0:T(128)S(1)} %add_rsqrt_fusion) | copy-start | bytes 1540
  232.6 149.2 %all-to-all-start.1 = ((bf16[32,2,24576]{2,1,0:T(2,128)(2,1)}), bf16[32,2,24576]{2,1,0:T(2,128)(2,1)}, u32[]{:S(2)}, u32[]{:S(2)}) async-start(bf16[32,2,24576]{2,1,0:T(2,128)(2,1)} %reshape.167), calls=%async_computation.1 | async-start | bytes 6291456 | tf_op jit(solution)/shard_map/all_to_all | solution.py:45
  400.8 5.5 copy-start.11
  400.8 5.5 copy-start.13
  406.2 6.4 copy-start.12
  406.2 6.4 copy-start.10
  416.2 148.7 %all-to-all-start.2 = ((bf16[32,24,2048]{2,1,0:T(8,128)(2,1)}), bf16[32,24,2048]{2,1,0:T(8,128)(2,1)}, u32[]{:S(2)}, u32[]{:S(2)}) async-start(bf16[32,24,2048]{2,1,0:T(8,128)(2,1)} %bitcast.136), calls=%async_computation.2 | async-start | bytes 6291456 | tf_op jit(solution)/shard_map/all_to_all | solution.py:53
  565.0 148.9 %all-to-all-start.3 = ((bf16[32,24,2048]{2,1,0:T(8,128)(2,1)}), bf16[32,24,2048]{2,1,0:T(8,128)(2,1)}, u32[]{:S(2)}, u32[]{:S(2)}) async-start(bf16[32,24,2048]{2,1,0:T(8,128)(2,1)} %bitcast.135), calls=%async_computation.3 | async-start | bytes 6291456 | tf_op jit(solution)/shard_map/all_to_all | solution.py:49
  572.7 329.4 %all-reduce.2.cloned.1.call-start = ((), (), s32[]{:S(2)}) async-start(), calls=%async_computation.4 | async-start | bytes 131072 | tf_op jit(solution)/shard_map/psum | solution.py:146
  716.3 0.8 copy-start.9
  716.3 1.9 copy-start.1
  716.8 3.5 copy-start.4
  716.8 3.5 copy-start.7
  718.2 4.2 copy-start.3
  718.2 4.2 copy-start.8
Sparse Core Ops, SparseCore 0:
  722.5 179.5 all-reduce.1
where the time goes:
time: 914 us; the launch traced here: 910 us
  waiting for transfers between devices  612 us (67%)
  local copies, waits for them, and re-layouts  96.6 us (11%)
  other arithmetic  53.5 us (6%)
  starting transfers between devices  50.6 us (6%)
  blocking collectives  48.8 us (5%)
  matrix products  33.5 us (4%)
  between operations  15 us (2%)
    all_to_all x2, waiting for transfers between devices, deliver(): lax.all_to_all(doubled, 'expert', split_axis=1, concat_axis=1, tiled=True)  187 us
    all_to_all x1, waiting for transfers between devices, send_backs(): lax.all_to_all(expert_back, 'expert', split_axis=0, concat_axis=0, tiled=...  137 us
    all_to_all x1, waiting for transfers between devices, send_outputs(): lax.all_to_all(expert_out, 'expert', split_axis=0, concat_axis=0, tiled=T...  135 us
    psum x1, waiting for transfers between devices, per_device(): lax.psum(router_term.astype(jnp.bfloat16), 'expert').astype(jnp.float32)  129 us
    unnamed x34, local copies, waits for them, and re-layouts  57 us
    psum x1, blocking collectives, per_device(): lax.psum(gain_contribution.astype(jnp.bfloat16), 'expert')  48.8 us
    unnamed x2, other arithmetic  41.1 us
    broadcast_in_dim x6, local copies, waits for them, and re-layouts, deliver(): jnp.broadcast_to(shaped, (stack_count, expert_count, 2, capacity * model_...  38.4 us
  transfers between devices with their start and end apart: 7, of which 7 were waited for; matrix products, arithmetic and copies ran while one was open for 10% of the time, Pallas kernels for 0%

commit v1 on v0

v1 whole, which is shorter than its diff:
```python
import functools

import jax
import jax.numpy as jnp
from jax import lax
from jax.experimental import pallas as pl
from jax.experimental.pallas import tpu as pltpu
from jax.sharding import PartitionSpec as P

EPSILON = 1e-05
LANES = 128
MESH = pl.DeviceIdType.MESH
F32 = jnp.float32
BF16 = jnp.bfloat16


def from_behind(value, axis, steps):
    count = lax.axis_size(axis)
    pairs = [(source, (source + steps) % count) for source in range(count)]
    return lax.ppermute(value, axis, pairs)


def dot(a, b, contract=(1, 0)):
    return lax.dot_general(
        a, b, (((contract[0],), (contract[1],)), ((), ())), preferred_element_type=F32
    )


def split(value):
    high = value.astype(BF16)
    return high, (value - high.astype(F32)).astype(BF16)


def kernel(
    nz,
    cap,
    disp,
    normed,
    arriving,
    returned,
    inv,
    gain,
    picks,
    targets,
    gates,
    router_t,
    gate_hbm,
    up_hbm,
    down_hbm,
    lig,
    totals,
    gate_w,
    up_w,
    down_w,
    buf,
    own,
    psend,
    precv,
    own_share,
    share_send,
    share_recv,
    rsend,
    ret,
    ssend,
    sret,
    weights,
    stage,
    q_src,
    q_dst,
    x_src,
    x_dst,
    a_src,
    a_dst,
    w_sem,
    l_sem,
    d_send,
    d_recv,
    f_send,
    f_recv,
    p_send,
    p_recv,
    h_send,
    h_recv,
    r_send,
    r_recv,
    s_send,
    s_recv,
    q_send,
    q_recv,
    x_send,
    x_recv,
    a_send,
    a_recv,
):
    steps = nz // 2
    half_width = gate_w.shape[1]
    width = gate_w.shape[0]
    half_model = width // 2
    rows = normed.shape[0]
    section = lax.axis_index("section")
    me = lax.axis_index("expert")
    chip = me // 2
    core = me - chip * 2
    sibling = chip * 2 + 1 - core

    def at_offset(offset):
        return lax.rem(chip + offset + nz, nz) * 2 + core

    def remote(src, dst, send, recv, target):
        return pltpu.make_async_remote_copy(
            src_ref=src,
            dst_ref=dst,
            send_sem=send,
            recv_sem=recv,
            device_id=(section, target),
            device_id_type=MESH,
        )

    def offset_of(step, side):
        if side == 0:
            return steps - step
        return lax.rem(steps + step, nz) if not isinstance(step, int) else (steps + step) % nz

    def dispatch(step, side):
        offset = offset_of(step, side)
        target = at_offset(offset)
        return remote(
            disp.at[target // 2],
            buf.at[step, side],
            d_send.at[step, side],
            d_recv.at[step, side],
            target,
        )

    def forward(step, side):
        return remote(
            buf.at[step, side],
            buf.at[step, 2 + side],
            f_send.at[step, side],
            f_recv.at[step, side],
            sibling,
        )

    def partial(step):
        return remote(psend.at[step], precv.at[step], p_send.at[step], p_recv.at[step], sibling)

    def partial_share(step):
        return remote(
            share_send.at[step], share_recv.at[step], h_send.at[step], h_recv.at[step], sibling
        )

    def give_back(step, side):
        target = at_offset(-offset_of(step, side))
        return remote(
            rsend.at[step, side],
            ret.at[chip],
            r_send.at[step, side],
            r_recv.at[step, side],
            target,
        )

    def give_share(step, side):
        target = at_offset(-offset_of(step, side))
        return remote(
            ssend.at[step, side],
            sret.at[chip],
            s_send.at[step, side],
            s_recv.at[step, side],
            target,
        )

    barrier = pltpu.get_barrier_semaphore()

    def greet(offset, carry):
        pl.semaphore_signal(
            barrier, inc=1, device_id=(section, at_offset(offset)), device_id_type=MESH
        )
        return carry

    lax.fori_loop(1, nz, greet, 0)
    pl.semaphore_signal(barrier, inc=1, device_id=(section, sibling), device_id_type=MESH)
    pl.semaphore_wait(barrier, nz)

    def send_both(step, carry):
        dispatch(step, 0).start()

        @pl.when(step > 0)
        def _():
            dispatch(step, 1).start()

        return carry

    lax.fori_loop(0, steps, send_both, 0)
    self_copy = pltpu.make_async_copy(disp.at[chip], buf.at[0, 1], l_sem.at[0])
    self_copy.start()
    loads = [
        pltpu.make_async_copy(gate_hbm, gate_w, w_sem.at[0]),
        pltpu.make_async_copy(up_hbm, up_w, w_sem.at[1]),
        pltpu.make_async_copy(down_hbm, down_w, w_sem.at[2]),
    ]
    for load in loads:
        load.start()

    slots = lax.broadcasted_iota(jnp.int32, (rows, nz * 2 * cap), 1)
    for part in range(2):
        mix = jnp.where(slots == targets[:, 0:1] + part * cap, gates[:, 0:1], 0.0)
        mix = mix + jnp.where(slots == targets[:, 1:2] + part * cap, gates[:, 1:2], 0.0)
        high, low = split(mix)
        weights[part, 0:rows, :] = high
        weights[part, rows : 2 * rows, :] = low
    stage[...] = jnp.zeros_like(stage)

    self_copy.wait()
    for load in loads:
        load.wait()

    def receive(step):
        for side in range(2):
            if side == 0:
                dispatch(step, side).wait_recv()
            else:

                @pl.when(step > 0)
                def _():
                    dispatch(step, 1).wait_recv()

            forward(step, side).start()

    def compute(step):
        for side in range(2):
            forward(step, side).wait_recv()
        block = buf[step].reshape(8 * cap, width)

        def part(value, which):
            return value.reshape(4, 2 * cap, half_width)[:, which * cap : (which + 1) * cap].reshape(
                4 * cap, half_width
            )

        gate_pre = part(dot(block, gate_w[...]), 0)
        up_pre = part(dot(block, up_w[...]), 0)
        hidden_grad = part(dot(block, down_w[...], (1, 1)), 1)
        logistic = jax.nn.sigmoid(gate_pre)
        activated = gate_pre * logistic
        share = jnp.sum(activated * up_pre * hidden_grad, axis=1, keepdims=True)
        diagonal = lax.broadcasted_iota(jnp.int32, (cap, LANES), 0) == lax.broadcasted_iota(
            jnp.int32, (cap, LANES), 1
        )
        for which in range(4):
            column = share[which * cap : (which + 1) * cap]
            line = jnp.sum(jnp.where(diagonal, column, 0.0), axis=0, keepdims=True)
            tile = jnp.broadcast_to(line, (8, LANES))
            if which < 2:
                own_share[step, which] = tile
            else:
                share_send[step, which - 2] = tile
        partial_share(step).start()
        gate_grad = (
            hidden_grad * up_pre * logistic * (1.0 + gate_pre * (1.0 - logistic))
        ).astype(BF16)
        up_grad = (hidden_grad * activated).astype(BF16)
        chunk = min(512, width)
        for start in range(0, width, chunk):
            columns = slice(start, start + chunk)
            back = dot(gate_grad, gate_w[columns, :], (1, 1)) + dot(
                up_grad, up_w[columns, :], (1, 1)
            )
            own[step, :, columns] = back[: 2 * cap]
            psend[step, :, columns] = back[2 * cap :].astype(BF16)
        partial(step).start()

    def finish(step):
        partial_share(step).wait_recv()
        for side in range(2):
            ssend[step, side] = own_share[step, side] + share_recv[step, side]
        partial(step).wait_recv()
        total = own[step] + precv[step].astype(F32)
        for side in range(2):
            mine = total[side * cap : (side + 1) * cap]
            stacked = jnp.concatenate([mine[:, :half_model], mine[:, half_model:]], axis=0)
            rsend[step, side] = stacked.astype(BF16)
        for side in range(2):
            if side == 0:
                give_share(step, side).start()
                give_back(step, side).start()
            else:

                @pl.when(step > 0)
                def _():
                    give_share(step, 1).start()
                    give_back(step, 1).start()

    def pipeline(turn, carry):
        @pl.when(turn < steps)
        def _():
            receive(turn)

        @pl.when((turn >= 1) & (turn <= steps))
        def _():
            compute(turn - 1)

        @pl.when(turn >= 2)
        def _():
            finish(turn - 2)

        return carry

    lax.fori_loop(0, steps + 2, pipeline, 0)
    self_back = pltpu.make_async_copy(rsend.at[0, 1], ret.at[chip], l_sem.at[1])
    self_share = pltpu.make_async_copy(ssend.at[0, 1], sret.at[chip], l_sem.at[2])
    self_back.start()
    self_share.start()
    self_back.wait()
    self_share.wait()

    def wait_share(step, carry):
        give_share(step, 0).wait_recv()

        @pl.when(step > 0)
        def _():
            give_share(step, 1).wait_recv()

        return carry

    lax.fori_loop(0, steps, wait_share, 0)
    shares = jnp.max(sret[...], axis=1)
    expert_ids = lax.broadcasted_iota(jnp.int32, (rows, nz), 1)
    places = lax.broadcasted_iota(jnp.int32, (rows, LANES), 1)
    share_parts = split(shares)
    share_parts = share_parts + ((shares - share_parts[0].astype(F32) - share_parts[1].astype(F32)).astype(BF16),)
    gate_share = []
    for k in range(2):
        pick = picks[:, k : k + 1]
        onehot = (expert_ids == pick).astype(BF16)
        line = dot(onehot, share_parts[0]) + dot(onehot, share_parts[1]) + dot(onehot, share_parts[2])
        place = targets[:, k : k + 1] - pick * (2 * cap)
        gate_share.append(
            jnp.sum(jnp.where(places == place, line, 0.0), axis=1, keepdims=True)
        )
    mean_share = gates[:, 0:1] * gate_share[0] + gates[:, 1:2] * gate_share[1]
    logit_grad = jnp.zeros((rows, nz), F32)
    for k in range(2):
        select_grad = gates[:, k : k + 1] * (gate_share[k] - mean_share)
        logit_grad = logit_grad + jnp.where(expert_ids == picks[:, k : k + 1], select_grad, 0.0)
    grad_high, grad_low = split(logit_grad)
    router_part = dot(grad_high, router_t[...]) + dot(grad_low, router_t[...])
    router_term = dot(grad_high, normed[...], (0, 0)) + dot(grad_low, normed[...], (0, 0))
    blocks = width // LANES
    for block in range(blocks):
        stage[:, block, :] = router_term[:, block * LANES : (block + 1) * LANES]

    def wait_back(step, carry):
        give_back(step, 0).wait_recv()

        @pl.when(step > 0)
        def _():
            give_back(step, 1).wait_recv()

        return carry

    lax.fori_loop(0, steps, wait_back, 0)
    came_back = ret[...].reshape(nz * 2 * cap, half_model)
    moved = []
    for part in range(2):
        both = dot(weights[part], came_back)
        moved.append(both[:rows] + both[rows:])
    normed_grad = jnp.concatenate(moved, axis=1) + router_part
    unit = arriving[...].astype(F32) * inv[...]
    gain_term = jnp.sum(normed_grad * unit, axis=0, keepdims=True)
    for block in range(nz):
        stage[block, blocks : blocks + 1, :] = gain_term[:, block * LANES : (block + 1) * LANES]
    q_src[...] = stage[...].astype(BF16)

    def reduce_copy(offset):
        target = at_offset(offset)
        return remote(
            q_src.at[target // 2], q_dst.at[offset], q_send.at[offset], q_recv.at[offset], target
        )

    def gather_copy(offset):
        return remote(
            a_src, a_dst.at[chip], a_send.at[offset], a_recv.at[offset], at_offset(offset)
        )

    def start_reduce(offset, carry):
        reduce_copy(offset).start()
        return carry

    lax.fori_loop(1, nz, start_reduce, 0)
    self_reduce = pltpu.make_async_copy(q_src.at[chip], q_dst.at[0], l_sem.at[3])
    self_reduce.start()

    scaled = normed_grad * gain[...].astype(F32)
    mean_scaled = jnp.mean(scaled * unit, axis=-1, keepdims=True)
    lig[...] = (returned[...].astype(F32) + inv[...] * (scaled - unit * mean_scaled)).astype(BF16)

    def wait_reduce(offset, carry):
        reduce_copy(offset).wait_recv()
        return carry

    self_reduce.wait()
    lax.fori_loop(1, nz, wait_reduce, 0)
    x_src[...] = jnp.sum(q_dst[...].astype(F32), axis=0)
    across = remote(x_src, x_dst, x_send.at[0], x_recv.at[0], sibling)
    across.start()
    across.wait_recv()
    a_src[...] = (x_src[...] + x_dst[...]).astype(BF16)

    def start_gather(offset, carry):
        gather_copy(offset).start()
        return carry

    lax.fori_loop(1, nz, start_gather, 0)
    self_gather = pltpu.make_async_copy(a_src, a_dst.at[chip], l_sem.at[4])
    self_gather.start()
    self_gather.wait()

    def drain(step, carry):
        dispatch(step, 0).wait_send()
        forward(step, 0).wait_send()
        forward(step, 1).wait_send()
        partial(step).wait_send()
        partial_share(step).wait_send()
        give_back(step, 0).wait_send()
        give_share(step, 0).wait_send()

        @pl.when(step > 0)
        def _():
            dispatch(step, 1).wait_send()
            give_back(step, 1).wait_send()
            give_share(step, 1).wait_send()

        return carry

    lax.fori_loop(0, steps, drain, 0)
    across.wait_send()

    def wait_gather(offset, carry):
        reduce_copy(offset).wait_send()
        gather_copy(offset).wait()
        return carry

    lax.fori_loop(1, nz, wait_gather, 0)
    totals[...] = a_dst[...].astype(F32)


def exchange(
    nz, cap, disp, normed, arriving, returned, inv, gain, picks, targets, gates, router_t, gate, up, down
):
    steps = nz // 2
    rows, width = normed.shape
    half_width = gate.shape[1]
    lines = -(-(width // LANES + 1) // 16) * 16
    vmem = pl.BlockSpec(memory_space=pltpu.VMEM)
    anywhere = pl.BlockSpec(memory_space=pl.ANY)
    dma = pltpu.SemaphoreType.DMA
    scratch = [
        pltpu.VMEM((width, half_width), BF16),
        pltpu.VMEM((width, half_width), BF16),
        pltpu.VMEM((half_width, width), BF16),
        pltpu.VMEM((steps, 4, 2 * cap, width), BF16),
        pltpu.VMEM((steps, 2 * cap, width), F32),
        pltpu.VMEM((steps, 2 * cap, width), BF16),
        pltpu.VMEM((steps, 2 * cap, width), BF16),
        pltpu.VMEM((steps, 2, 8, LANES), F32),
        pltpu.VMEM((steps, 2, 8, LANES), F32),
        pltpu.VMEM((steps, 2, 8, LANES), F32),
        pltpu.VMEM((steps, 2, 2 * cap, width // 2), BF16),
        pltpu.VMEM((nz, 2 * cap, width // 2), BF16),
        pltpu.VMEM((steps, 2, 8, LANES), F32),
        pltpu.VMEM((nz, 8, LANES), F32),
        pltpu.VMEM((2, 2 * rows, nz * 2 * cap), BF16),
        pltpu.VMEM((nz, lines, LANES), F32),
        pltpu.VMEM((nz, lines, LANES), BF16),
        pltpu.VMEM((nz, lines, LANES), BF16),
        pltpu.VMEM((lines, LANES), F32),
        pltpu.VMEM((lines, LANES), F32),
        pltpu.VMEM((lines, LANES), BF16),
        pltpu.VMEM((nz, lines, LANES), BF16),
        dma((3,)),
        dma((5,)),
        dma((steps, 2)),
        dma((steps, 2)),
        dma((steps, 2)),
        dma((steps, 2)),
        dma((steps,)),
        dma((steps,)),
        dma((steps,)),
        dma((steps,)),
        dma((steps, 2)),
        dma((steps, 2)),
        dma((steps, 2)),
        dma((steps, 2)),
        dma((nz,)),
        dma((nz,)),
        dma((1,)),
        dma((1,)),
        dma((nz,)),
        dma((nz,)),
    ]
    return pl.pallas_call(
        functools.partial(kernel, nz, cap),
        out_shape=(
            jax.ShapeDtypeStruct((rows, width), BF16),
            jax.ShapeDtypeStruct((nz, lines, LANES), F32),
        ),
        in_specs=[vmem] * 10 + [anywhere] * 3,
        out_specs=(vmem, vmem),
        scratch_shapes=scratch,
        compiler_params=pltpu.CompilerParams(
            collective_id=0, has_side_effects=True, vmem_limit_bytes=52 * 1024 * 1024
        ),
        cost_estimate=pl.CostEstimate(
            flops=8_000_000_000, bytes_accessed=8_000_000, transcendentals=200_000
        ),
    )(disp, normed, arriving, returned, inv, gain, picks, targets, gates, router_t, gate, up, down)


def per_device(
    activations,
    cotangents,
    norm_gain,
    routes,
    lengths,
    router_weight,
    gate_weight,
    up_weight,
    down_weight,
):
    arriving = from_behind(activations, "section", 1)[0]
    returned = from_behind(cotangents, "section", -1)[0]
    rows, width = arriving.shape
    experts = router_weight.shape[2]
    top = routes.shape[2]
    cap = 3 * rows * top // (2 * experts)
    picks = routes[0]
    expert_ids = jnp.arange(experts, dtype=jnp.int32)
    onehot = picks[:, :, None] == expert_ids[None, None, :]
    live = (jnp.arange(rows, dtype=jnp.int32) < lengths[0, 0])[:, None]
    hot = (jnp.any(onehot, axis=1) & live).astype(BF16)
    order = jnp.arange(rows, dtype=jnp.int32)
    earlier = (order[:, None] > order[None, :]).astype(BF16)
    before = dot(earlier, hot)
    place = jnp.sum(jnp.where(onehot, before[:, None, :], 0.0), axis=2).astype(jnp.int32)
    targets = jnp.where(live, picks * (2 * cap) + place, -4 * cap)
    slots = jnp.arange(experts * 2 * cap, dtype=jnp.int32)
    select_x = jnp.any(targets[:, :, None] == slots[None, None, :], axis=1)
    select_g = jnp.any(targets[:, :, None] + cap == slots[None, None, :], axis=1)
    full = arriving.astype(F32)
    inv = lax.rsqrt(jnp.mean(full * full, axis=-1, keepdims=True) + EPSILON)
    normed = (full * inv * norm_gain[0].astype(F32)).astype(BF16)
    disp = dot(
        jnp.concatenate([select_x, select_g], axis=0).astype(BF16),
        jnp.concatenate([normed, returned], axis=0),
        (0, 0),
    ).astype(BF16)
    disp = disp.reshape(experts, 2 * cap, width)
    logits = jnp.dot(normed, router_weight[0], preferred_element_type=F32)
    chosen = jnp.sum(jnp.where(onehot, logits[:, None, :], 0.0), axis=2)
    gates = 1.0 / jnp.sum(jnp.exp(chosen[:, None, :] - chosen[:, :, None]), axis=2)
    lig, totals = exchange(
        experts,
        cap,
        disp,
        normed,
        arriving,
        returned,
        inv,
        norm_gain,
        picks,
        targets,
        gates,
        router_weight[0].T,
        gate_weight[0, 0],
        up_weight[0, 0],
        down_weight[0, 0],
    )
    blocks = width // LANES
    router_grad = totals[:, :blocks, :].reshape(experts, width).T
    gain_grad = totals[:, blocks, :].reshape(width)
    return (lig[None], router_grad[None], gain_grad[None])


def solution(mesh):
    in_specs = (
        P("section", "expert", None),
        P("section", "expert", None),
        P("section", None),
        P("section", "expert", None),
        P("section", "expert"),
        P("section", None, None),
        P("section", "expert", None, None),
        P("section", "expert", None, None),
        P("section", "expert", None, None),
    )
    out_specs = (P("section", "expert", None), P("section", None, None), P("section", None))
    return jax.shard_map(
        per_device, mesh=mesh, in_specs=in_specs, out_specs=out_specs, check_vma=False
    )
```

time: 914 us -> 278 us (0.30)
  waiting for transfers between devices: 612 us -> 2.46 us
  Pallas kernels: 0 us -> 255 us
  local copies, waits for them, and re-layouts: 96.6 us -> 3.45 us
  other arithmetic: 53.5 us -> 1.51 us
  blocking collectives: 48.8 us -> 0 us
  starting transfers between devices: 50.6 us -> 9.59 us
  matrix products: 33.5 us -> 3.99 us
  between operations: 15 us -> 1.4 us
    all_to_all x4 -> x0, waiting for transfers between devices: 459 us -> none  [the longest x2 187 us: deliver(): lax.all_to_all(doubled, 'expert', split_axis=1, concat_axis=1, tiled=True)]
    pallas_call x0 -> x1, Pallas kernels: none -> 255 us  [exchange(): pl.pallas_call(functools.partial(kernel, nz, cap), out_shape=(jax.ShapeDt...]
    psum x1 -> x0, waiting for transfers between devices: 129 us -> none  [per_device(): lax.psum(router_term.astype(jnp.bfloat16), 'expert').astype(jnp.float32)]
    unnamed x34 -> x11, local copies, waits for them, and re-layouts: 57 us -> 2.3 us
    psum x1 -> x0, blocking collectives: 48.8 us -> none  [per_device(): lax.psum(gain_contribution.astype(jnp.bfloat16), 'expert')]
    unnamed x2 -> x0, other arithmetic: 41.1 us -> none
    all_to_all x4 -> x0, starting transfers between devices: 40.4 us -> none  [the longest x2 25 us: deliver(): lax.all_to_all(doubled, 'expert', split_axis=1, concat_axis=1, tiled=True)]
    broadcast_in_dim x10 -> x0, local copies, waits for them, and re-layouts: 38.7 us -> none  [the longest x6 38.4 us: deliver(): jnp.broadcast_to(shaped, (stack_count, expert_count, 2, capacity * model_...]
  transfers between devices with their start and end apart: 7 -> 2, of which waited for: 7 -> 1; matrix products, arithmetic and copies ran while one was open for 10% -> 1% of each run, Pallas kernels for 0% -> 0%
where the time goes in v1:
time: 278 us
  Pallas kernels  255 us (92%)
  starting transfers between devices  9.59 us (3%)
  matrix products  3.99 us (1%)
  local copies, waits for them, and re-layouts  3.45 us (1%)
    pallas_call x1, Pallas kernels, exchange(): pl.pallas_call(functools.partial(kernel, nz, cap), out_shape=(jax.ShapeDt...  255 us
    ppermute x2, starting transfers between devices, from_behind(): return lax.ppermute(value, axis, pairs)  9.59 us
  transfers between devices with their start and end apart: 2, of which 1 were waited for; matrix products, arithmetic and copies ran while one was open for 1% of the time, Pallas kernels for 0%

profile of v1, /device:TPU:1, one launch (start us, length us, event | category | flops | bytes accessed | tf_op | source)
XLA Modules:
  0.0 277.5 jit_solution(660244663578876224)
XLA Ops:
  0.6 4.0 %collective-permute-start = (bf16[1,128,2048]{2,1,0:T(8,128)(2,1)}, bf16[1,128,2048]{2,1,0:T(8,128)(2,1)S(1)}, u32[]{:S(2)}, u32[]{:S(2)}) collective-permute-start(bf16[1,128,2048]{2,1,0:T(8,128)(2,1)} %param.9), channel_id=1, source_target_pairs={{0,32},{32,64},{64,96},{96,128},{128,160},{160,192},{192,224},{224... | collective-permute-start | bytes 1572872 | tf_op jit(solution)/shard_map/ppermute | solution.py:20
  4.7 5.6 %collective-permute-start.1 = (bf16[1,128,2048]{2,1,0:T(8,128)(2,1)}, bf16[1,128,2048]{2,1,0:T(8,128)(2,1)S(1)}, u32[]{:S(2)}, u32[]{:S(2)}) collective-permute-start(bf16[1,128,2048]{2,1,0:T(8,128)(2,1)} %param.10), channel_id=1, source_target_pairs={{0,480},{32,0},{64,32},{96,64},{128,96},{160,128},{192,160},{224,1... | collective-permute-start | bytes 1572872 | tf_op jit(solution)/shard_map/ppermute | solution.py:20
  10.9 0.7 mul.60
  11.6 0.8 copy.23
  12.4 0.1 copy.24
  12.5 0.1 fusion.17
  12.6 2.5 collective-permute-done
  15.1 0.0 copy-start.2
  15.1 0.2 fusion
  15.3 1.2 fusion.12
  16.5 0.1 copy.25
  16.6 0.1 copy.30
  16.7 0.1 broadcast_add_fusion
  16.8 0.1 copy.28
  16.9 0.1 copy.26
  17.0 0.2 fusion.6
  17.2 0.1 copy.31.inv
  17.3 0.2 fusion.2.normed
  17.5 0.0 collective-permute-done.1
  17.5 0.0 copy-start.3
  17.5 0.0 copy-start
  17.6 0.0 copy-start.1
  17.6 2.7 convolution_convert_fusion
  20.3 0.0 copy-done.2
  20.3 0.0 copy-done.3
  20.3 0.0 copy-done
  20.3 0.0 copy-done.1
  20.3 255.1 %shard_map.112 = (bf16[128,2048]{1,0:T(8,128)(2,1)S(1)}, f32[16,32,128]{2,1,0:T(8,128)S(1)}) custom-call(bf16[16,48,2048]{2,1,0:T(8,128)(2,1)} %bitcast.40, bf16[128,2048]{1,0:T(8,128)(2,1)S(1)} %fusion.2.normed, bf16[128,2048]{1,0:T(8,128)(2,1)} %bitcast.41, bf16[128,2048]{1,0:T(8,128)(2,1)} %bitcast.43, f32[128,1]{1,0:T(8,128)S(1)} %copy.31.inv, ...), custom_call_target="tpu_custom_call" | custom-call | flops 8000000000 | bytes 8000000 | tf_op jit(solution)/shard_map/pallas_call | solution.py:500
  275.4 0.6 slice_bitcast_fusion
  276.0 0.7 copy.34
  276.7 0.8 copy.37
  (8 shorter events, 0.1 us)
Async XLA Ops:
  0.6 14.4 %collective-permute-start = (bf16[1,128,2048]{2,1,0:T(8,128)(2,1)}, bf16[1,128,2048]{2,1,0:T(8,128)(2,1)S(1)}, u32[]{:S(2)}, u32[]{:S(2)}) collective-permute-start(bf16[1,128,2048]{2,1,0:T(8,128)(2,1)} %param.9), channel_id=1, source_target_pairs={{0,32},{32,64},{64,96},{96,128},{128,160},{160,192},{192,224},{224... | collective-permute-start | bytes 1572872 | tf_op jit(solution)/shard_map/ppermute | solution.py:20
  4.7 12.8 %collective-permute-start.1 = (bf16[1,128,2048]{2,1,0:T(8,128)(2,1)}, bf16[1,128,2048]{2,1,0:T(8,128)(2,1)S(1)}, u32[]{:S(2)}, u32[]{:S(2)}) collective-permute-start(bf16[1,128,2048]{2,1,0:T(8,128)(2,1)} %param.10), channel_id=1, source_target_pairs={{0,480},{32,0},{64,32},{96,64},{128,96},{160,128},{192,160},{224,1... | collective-permute-start | bytes 1572872 | tf_op jit(solution)/shard_map/ppermute | solution.py:20
  15.1 5.2 %copy-start.2 = (bf16[1,128,2048]{2,1,0:T(8,128)(2,1)}, bf16[1,128,2048]{2,1,0:T(8,128)(2,1)S(1)}, u32[]{:S(2)}) copy-start(bf16[1,128,2048]{2,1,0:T(8,128)(2,1)S(1)} %collective-permute-done) | copy-start | bytes 1572868
  17.5 2.7 copy-start.3
  17.5 2.7 copy-start
  17.6 2.7 copy-start.1

commit v2 on v0

v2 whole, which is shorter than its diff:
```python
import functools
import types

import jax
import jax.numpy as jnp
from jax import lax
from jax.experimental import pallas as pl
from jax.experimental.pallas import tpu as pltpu
from jax.sharding import PartitionSpec as P

EPSILON = 1e-05
LANES = 128
G_PIECES = 4
X_PIECES = 1
MESH = pl.DeviceIdType.MESH
F32 = jnp.float32
BF16 = jnp.bfloat16


def dot(a, b, contract=(1, 0)):
    return lax.dot_general(
        a, b, (((contract[0],), (contract[1],)), ((), ())), preferred_element_type=F32
    )


def split(value):
    high = value.astype(BF16)
    return high, (value - high.astype(F32)).astype(BF16)


def iota(shape, dim):
    return lax.broadcasted_iota(jnp.int32, shape, dim)


def kernel(nz, cap, sections, names, *refs):
    r = types.SimpleNamespace(**dict(zip(names, refs)))
    steps = nz // 2
    width, half_width = r.gate_w.shape
    half_model = width // 2
    rows = r.normed.shape[0]
    g_wide = half_model // G_PIECES
    x_wide = half_model // X_PIECES
    blocks = width // LANES
    section = lax.axis_index("section")
    me = lax.axis_index("expert")
    chip = me // 2
    core = me - chip * 2
    sibling = chip * 2 + 1 - core
    section_before = lax.rem(section + sections - 1, sections)
    section_after = lax.rem(section + 1, sections)

    def at_offset(offset):
        return lax.rem(chip + offset + nz, nz) * 2 + core

    def remote(src, dst, sems, index, target, home=section):
        return pltpu.make_async_remote_copy(
            src_ref=src,
            dst_ref=dst,
            send_sem=sems[0].at[index],
            recv_sem=sems[1].at[index],
            device_id=(home, target),
            device_id_type=MESH,
        )

    def offset_of(step, side):
        return steps - step if side == 0 else lax.rem(steps + step, nz)

    def hand_on(part, piece):
        columns = pl.ds((2 * piece + part) * x_wide, x_wide)
        return remote(
            r.acts.at[0, :, columns],
            r.xex.at[piece, pl.ds(part * rows, rows), :],
            (r.xe_send, r.xe_recv),
            2 * piece + part,
            me,
            section_after,
        )

    def hand_back(part, piece):
        columns = pl.ds((2 * piece + part) * g_wide, g_wide)
        return remote(
            r.cots.at[0, :, columns],
            r.gex.at[piece, pl.ds(part * rows, rows), :],
            (r.ge_send, r.ge_recv),
            2 * piece + part,
            me,
            section_before,
        )

    def dispatch_g(piece, step, side):
        target = at_offset(offset_of(step, side))
        return remote(
            r.dispg.at[piece, target // 2],
            r.gbuf.at[step, side, piece],
            (r.gd_send, r.gd_recv),
            (piece, step, side),
            target,
        )

    def dispatch_x(piece, step, side):
        target = at_offset(offset_of(step, side))
        return remote(
            r.dispx.at[piece, target // 2],
            r.xbuf.at[step, side, piece],
            (r.xd_send, r.xd_recv),
            (piece, step, side),
            target,
        )

    def forward_g(step, side):
        return remote(
            r.gbuf.at[step, side],
            r.gbuf.at[step, 2 + side],
            (r.gf_send, r.gf_recv),
            (step, side),
            sibling,
        )

    def forward_x(step, side):
        return remote(
            r.xbuf.at[step, side],
            r.xbuf.at[step, 2 + side],
            (r.xf_send, r.xf_recv),
            (step, side),
            sibling,
        )

    def partial(step):
        return remote(r.psend.at[step], r.precv.at[step], (r.p_send, r.p_recv), step, sibling)

    def partial_share(step):
        return remote(
            r.share_send.at[step], r.share_recv.at[step], (r.h_send, r.h_recv), step, sibling
        )

    def give_back(step, side):
        target = at_offset(-offset_of(step, side))
        return remote(
            r.rsend.at[step, side], r.ret.at[chip], (r.r_send, r.r_recv), (step, side), target
        )

    def give_share(step, side):
        target = at_offset(-offset_of(step, side))
        return remote(
            r.ssend.at[step, side], r.sret.at[chip], (r.s_send, r.s_recv), (step, side), target
        )

    def reduce_router(offset):
        target = at_offset(offset)
        return remote(
            r.q_src.at[target // 2], r.q_dst.at[offset], (r.q_send, r.q_recv), offset, target
        )

    def gather_router(offset):
        return remote(
            r.a_src, r.a_dst.at[chip], (r.a_send, r.a_recv), offset, at_offset(offset)
        )

    def gather_gain(offset):
        return remote(
            r.n_src, r.n_dst.at[offset], (r.n_send, r.n_recv), offset, at_offset(offset)
        )

    def pairs(body):
        def both(step, carry):
            body(step, 0)

            @pl.when(step > 0)
            def _():
                body(step, 1)

            return carry

        lax.fori_loop(0, steps, both, 0)

    def others(body):
        def one(offset, carry):
            body(offset)
            return carry

        lax.fori_loop(1, nz, one, 0)

    loads = [
        pltpu.make_async_copy(r.gate_hbm, r.gate_w, r.w_sem.at[0]),
        pltpu.make_async_copy(r.up_hbm, r.up_w, r.w_sem.at[1]),
        pltpu.make_async_copy(r.down_hbm, r.down_w, r.w_sem.at[2]),
    ]
    for load in loads:
        load.start()

    live = iota((1, rows), 1) < r.lengths[...]
    named = [iota((nz, rows), 0) == r.picks[k : k + 1, :] for k in range(2)]
    hot = jnp.where((named[0] | named[1]) & live, 1.0, 0.0).astype(BF16)
    earlier = jnp.where(iota((rows, rows), 0) < iota((rows, rows), 1), 1.0, 0.0).astype(BF16)
    before = dot(hot, earlier)
    targets = []
    for k in range(2):
        place = jnp.sum(jnp.where(named[k], before, 0.0), axis=0, keepdims=True)
        slot = r.picks[k : k + 1, :] * (2 * cap) + place.astype(jnp.int32)
        targets.append(jnp.where(live, slot, -4 * cap))
    slots = iota((nz * 2 * cap, rows), 0)
    for part in range(2):
        chosen = (slots == targets[0] + part * cap) | (slots == targets[1] + part * cap)
        r.select[:, part * rows : (part + 1) * rows] = jnp.where(chosen, 1.0, 0.0).astype(BF16)

    barrier = pltpu.get_barrier_semaphore()

    def greet(offset):
        pl.semaphore_signal(
            barrier, inc=1, device_id=(section, at_offset(offset)), device_id_type=MESH
        )

    others(greet)
    for home, target in ((section, sibling), (section_before, me), (section_after, me)):
        pl.semaphore_signal(barrier, inc=1, device_id=(home, target), device_id_type=MESH)
    pl.semaphore_wait(barrier, nz + 2)

    for piece in range(G_PIECES):
        for part in range(2):
            hand_back(part, piece).start()
    for piece in range(X_PIECES):
        for part in range(2):
            hand_on(part, piece).start()

    own_copies = []
    for piece in range(G_PIECES):
        for part in range(2):
            hand_back(part, piece).wait_recv()
        spread = dot(r.select[...], r.gex[piece]).astype(BF16)
        r.dispg[piece] = spread.reshape(nz, 2 * cap, g_wide)
        pairs(lambda step, side, piece=piece: dispatch_g(piece, step, side).start())
        own_copies.append(
            pltpu.make_async_copy(
                r.dispg.at[piece, chip], r.gbuf.at[0, 1, piece], r.l_sem.at[len(own_copies)]
            )
        )
        own_copies[-1].start()

    for piece in range(X_PIECES):
        for part in range(2):
            hand_on(part, piece).wait_recv()

    def sides(ref, count):
        parts = [
            ref[piece, part * rows : (part + 1) * rows, :]
            for piece in range(count)
            for part in range(2)
        ]
        return jnp.concatenate(parts, axis=1)

    full = sides(r.xex, X_PIECES).astype(F32)
    inv = lax.rsqrt(jnp.mean(full * full, axis=-1, keepdims=True) + EPSILON)
    r.normed[...] = (full * inv * r.gain[...].astype(F32)).astype(BF16)
    for piece in range(X_PIECES):
        start = 2 * piece * x_wide
        both = jnp.concatenate(
            [r.normed[:, start : start + x_wide], r.normed[:, start + x_wide : start + 2 * x_wide]],
            axis=0,
        )
        spread = dot(r.select[...], both).astype(BF16)
        r.dispx[piece] = spread.reshape(nz, 2 * cap, x_wide)
        pairs(lambda step, side, piece=piece: dispatch_x(piece, step, side).start())
        own_copies.append(
            pltpu.make_async_copy(
                r.dispx.at[piece, chip], r.xbuf.at[0, 1, piece], r.l_sem.at[len(own_copies)]
            )
        )
        own_copies[-1].start()

    same = iota((rows, rows), 0) == iota((rows, rows), 1)

    def upright(line):
        return jnp.sum(jnp.where(same, line, 0), axis=1, keepdims=True)

    expert_ids = iota((rows, nz), 1)
    picked = [upright(r.picks[k : k + 1, :]) for k in range(2)]
    target_of = [upright(targets[k]) for k in range(2)]
    logits = dot(r.normed[...], r.router_t[...], (1, 1))
    scores = [
        jnp.sum(jnp.where(expert_ids == picked[k], logits, 0.0), axis=1, keepdims=True)
        for k in range(2)
    ]
    gates = [1.0 / (1.0 + jnp.exp(scores[1 - k] - scores[k])) for k in range(2)]
    across_slots = iota((rows, nz * 2 * cap), 1)
    for part in range(2):
        mix = jnp.where(across_slots == target_of[0] + part * cap, gates[0], 0.0)
        mix = mix + jnp.where(across_slots == target_of[1] + part * cap, gates[1], 0.0)
        r.weights[part * rows : (part + 1) * rows, :] = mix.astype(BF16)

    for copy in own_copies:
        copy.wait()
    for load in loads:
        load.wait()

    def pick_rows(value, part):
        return value.reshape(4, 2 * cap, half_width)[:, part * cap : (part + 1) * cap].reshape(
            4 * cap, half_width
        )

    def receive_g(step):
        for piece in range(G_PIECES):
            dispatch_g(piece, step, 0).wait_recv()
        forward_g(step, 0).start()

        @pl.when(step > 0)
        def _():
            for piece in range(G_PIECES):
                dispatch_g(piece, step, 1).wait_recv()

        forward_g(step, 1).start()

    def compute_g(step):
        for side in range(2):
            forward_g(step, side).wait_recv()
        total = jnp.zeros((4 * cap, half_width), F32)
        for piece in range(G_PIECES):
            block = r.gbuf[step, :, piece].reshape(8 * cap, g_wide)
            for part in range(2):
                start = (2 * piece + part) * g_wide
                down = r.down_w[:, start : start + g_wide]
                total = total + pick_rows(dot(block, down, (1, 1)), part)
        r.hidden_grad[step] = total

    def receive_x(step):
        for piece in range(X_PIECES):
            dispatch_x(piece, step, 0).wait_recv()
        forward_x(step, 0).start()

        @pl.when(step > 0)
        def _():
            for piece in range(X_PIECES):
                dispatch_x(piece, step, 1).wait_recv()

        forward_x(step, 1).start()

    diagonal = iota((cap, LANES), 0) == iota((cap, LANES), 1)

    def compute_x(step):
        for side in range(2):
            forward_x(step, side).wait_recv()
        gate_pre = jnp.zeros((4 * cap, half_width), F32)
        up_pre = jnp.zeros((4 * cap, half_width), F32)
        for piece in range(X_PIECES):
            block = r.xbuf[step, :, piece].reshape(8 * cap, x_wide)
            for part in range(2):
                start = (2 * piece + part) * x_wide
                columns = slice(start, start + x_wide)
                gate_pre = gate_pre + pick_rows(dot(block, r.gate_w[columns, :]), part)
                up_pre = up_pre + pick_rows(dot(block, r.up_w[columns, :]), part)
        hidden_grad = r.hidden_grad[step]
        logistic = jax.nn.sigmoid(gate_pre)
        activated = gate_pre * logistic
        share = jnp.sum(activated * up_pre * hidden_grad, axis=1, keepdims=True)
        for which in range(4):
            column = share[which * cap : (which + 1) * cap]
            line = jnp.sum(jnp.where(diagonal, column, 0.0), axis=0, keepdims=True)
            tile = jnp.broadcast_to(line, (8, LANES))
            if which < 2:
                r.own_share[step, which] = tile
            else:
                r.share_send[step, which - 2] = tile
        partial_share(step).start()
        gate_grad = (
            hidden_grad * up_pre * logistic * (1.0 + gate_pre * (1.0 - logistic))
        ).astype(BF16)
        up_grad = (hidden_grad * activated).astype(BF16)
        chunk = min(512, width)
        for start in range(0, width, chunk):
            columns = slice(start, start + chunk)
            back = dot(gate_grad, r.gate_w[columns, :], (1, 1)) + dot(
                up_grad, r.up_w[columns, :], (1, 1)
            )
            r.own[step, :, columns] = back[: 2 * cap]
            r.psend[step, :, columns] = back[2 * cap :].astype(BF16)
        partial(step).start()

    def finish(step):
        partial_share(step).wait_recv()
        for side in range(2):
            r.ssend[step, side] = r.own_share[step, side] + r.share_recv[step, side]
        give_share(step, 0).start()

        @pl.when(step > 0)
        def _():
            give_share(step, 1).start()

        partial(step).wait_recv()
        total = r.own[step] + r.precv[step].astype(F32)
        for side in range(2):
            mine = total[side * cap : (side + 1) * cap]
            stacked = jnp.concatenate([mine[:, :half_model], mine[:, half_model:]], axis=0)
            r.rsend[step, side] = stacked.astype(BF16)
        give_back(step, 0).start()

        @pl.when(step > 0)
        def _():
            give_back(step, 1).start()

    def pipeline_g(turn, carry):
        @pl.when(turn < steps)
        def _():
            receive_g(turn)

        @pl.when(turn >= 1)
        def _():
            compute_g(turn - 1)

        return carry

    def pipeline_x(turn, carry):
        @pl.when(turn < steps)
        def _():
            receive_x(turn)

        @pl.when((turn >= 1) & (turn <= steps))
        def _():
            compute_x(turn - 1)

        @pl.when(turn >= 2)
        def _():
            finish(turn - 2)

        return carry

    lax.fori_loop(0, steps + 1, pipeline_g, 0)
    lax.fori_loop(0, steps + 2, pipeline_x, 0)

    base = G_PIECES + X_PIECES
    self_back = pltpu.make_async_copy(r.rsend.at[0, 1], r.ret.at[chip], r.l_sem.at[base])
    self_share = pltpu.make_async_copy(r.ssend.at[0, 1], r.sret.at[chip], r.l_sem.at[base + 1])
    self_back.start()
    self_share.start()
    self_share.wait()
    pairs(lambda step, side: give_share(step, side).wait_recv())

    shares = jnp.max(r.sret[...], axis=1)
    places = iota((rows, LANES), 1)
    first, second = split(shares)
    third = (shares - first.astype(F32) - second.astype(F32)).astype(BF16)
    gate_share = []
    for k in range(2):
        onehot = jnp.where(expert_ids == picked[k], 1.0, 0.0).astype(BF16)
        line = dot(onehot, first) + dot(onehot, second) + dot(onehot, third)
        place = target_of[k] - picked[k] * (2 * cap)
        gate_share.append(jnp.sum(jnp.where(places == place, line, 0.0), axis=1, keepdims=True))
    mean_share = gates[0] * gate_share[0] + gates[1] * gate_share[1]
    logit_grad = jnp.zeros((rows, nz), F32)
    for k in range(2):
        select_grad = gates[k] * (gate_share[k] - mean_share)
        logit_grad = logit_grad + jnp.where(expert_ids == picked[k], select_grad, 0.0)
    grad_high, grad_low = split(logit_grad)
    router_term = dot(grad_high, r.normed[...], (0, 0)) + dot(grad_low, r.normed[...], (0, 0))
    for block in range(blocks):
        r.stage[:, block, :] = router_term[:, block * LANES : (block + 1) * LANES]
    r.q_src[...] = r.stage[...].astype(BF16)
    others(lambda offset: reduce_router(offset).start())
    self_reduce = pltpu.make_async_copy(r.q_src.at[chip], r.q_dst.at[0], r.l_sem.at[base + 2])
    self_reduce.start()
    router_part = dot(grad_high, r.router_t[...]) + dot(grad_low, r.router_t[...])

    self_back.wait()
    pairs(lambda step, side: give_back(step, side).wait_recv())
    came_back = r.ret[...].reshape(nz * 2 * cap, half_model)
    both = dot(r.weights[...], came_back)
    normed_grad = jnp.concatenate([both[:rows], both[rows:]], axis=1) + router_part
    unit = sides(r.xex, X_PIECES).astype(F32) * inv
    gain_term = jnp.sum(normed_grad * unit, axis=0, keepdims=True)
    for block in range(blocks):
        r.gain_stage[block : block + 1, :] = gain_term[:, block * LANES : (block + 1) * LANES]
    r.n_src[...] = r.gain_stage[...].astype(BF16)
    others(lambda offset: gather_gain(offset).start())
    r.n_dst[0] = r.n_src[...]

    self_reduce.wait()
    others(lambda offset: reduce_router(offset).wait_recv())
    r.x_src[...] = jnp.sum(r.q_dst[...].astype(F32), axis=0)
    across_router = remote(r.x_src, r.x_dst, (r.x_send, r.x_recv), 0, sibling)
    across_router.start()

    scaled = normed_grad * r.gain[...].astype(F32)
    mean_scaled = jnp.mean(scaled * unit, axis=-1, keepdims=True)
    returned = sides(r.gex, G_PIECES).astype(F32)
    r.lig[...] = (returned + inv * (scaled - unit * mean_scaled)).astype(BF16)

    across_router.wait_recv()
    r.a_src[...] = (r.x_src[...] + r.x_dst[...]).astype(BF16)
    others(lambda offset: gather_router(offset).start())
    r.a_dst[chip] = r.a_src[...]

    others(lambda offset: gather_gain(offset).wait_recv())
    r.y_src[...] = jnp.sum(r.n_dst[...].astype(F32), axis=0)
    across_gain = remote(r.y_src, r.y_dst, (r.x_send, r.x_recv), 1, sibling)
    across_gain.start()

    for piece in range(G_PIECES):
        for part in range(2):
            hand_back(part, piece).wait_send()
        pairs(lambda step, side, piece=piece: dispatch_g(piece, step, side).wait_send())
    for piece in range(X_PIECES):
        for part in range(2):
            hand_on(part, piece).wait_send()
        pairs(lambda step, side, piece=piece: dispatch_x(piece, step, side).wait_send())

    def drain(step, carry):
        for side in range(2):
            forward_g(step, side).wait_send()
            forward_x(step, side).wait_send()
        partial(step).wait_send()
        partial_share(step).wait_send()
        return carry

    lax.fori_loop(0, steps, drain, 0)
    pairs(lambda step, side: give_back(step, side).wait_send())
    pairs(lambda step, side: give_share(step, side).wait_send())
    others(lambda offset: reduce_router(offset).wait_send())
    others(lambda offset: gather_gain(offset).wait_send())

    across_router.wait_send()
    across_gain.wait()
    r.gain_total[...] = r.y_src[...] + r.y_dst[...]
    others(lambda offset: gather_router(offset).wait())
    for block in range(blocks):
        r.router_total[:, block * LANES : (block + 1) * LANES] = r.a_dst[:, block, :].astype(F32)


def exchange(nz, cap, sections, lengths, picks, gain, router_t, acts, cots, gate, up, down):
    steps = nz // 2
    rows, width = acts.shape[1:]
    half_width = gate.shape[1]
    half_model = width // 2
    lines = width // LANES
    g_wide = half_model // G_PIECES
    x_wide = half_model // X_PIECES
    vmem = pl.BlockSpec(memory_space=pltpu.VMEM)
    anywhere = pl.BlockSpec(memory_space=pl.ANY)

    def sems(*shape):
        return pltpu.SemaphoreType.DMA(shape)

    tall = -(-lines // 16) * 16
    scratch = {
        "gate_w": pltpu.VMEM((width, half_width), BF16),
        "up_w": pltpu.VMEM((width, half_width), BF16),
        "down_w": pltpu.VMEM((half_width, width), BF16),
        "select": pltpu.VMEM((nz * 2 * cap, 2 * rows), BF16),
        "gex": pltpu.VMEM((G_PIECES, 2 * rows, g_wide), BF16),
        "xex": pltpu.VMEM((X_PIECES, 2 * rows, x_wide), BF16),
        "normed": pltpu.VMEM((rows, width), BF16),
        "dispg": pltpu.VMEM((G_PIECES, nz, 2 * cap, g_wide), BF16),
        "dispx": pltpu.VMEM((X_PIECES, nz, 2 * cap, x_wide), BF16),
        "gbuf": pltpu.VMEM((steps, 4, G_PIECES, 2 * cap, g_wide), BF16),
        "xbuf": pltpu.VMEM((steps, 4, X_PIECES, 2 * cap, x_wide), BF16),
        "hidden_grad": pltpu.VMEM((steps, 4 * cap, half_width), F32),
        "own": pltpu.VMEM((steps, 2 * cap, width), F32),
        "psend": pltpu.VMEM((steps, 2 * cap, width), BF16),
        "precv": pltpu.VMEM((steps, 2 * cap, width), BF16),
        "own_share": pltpu.VMEM((steps, 2, 8, LANES), F32),
        "share_send": pltpu.VMEM((steps, 2, 8, LANES), F32),
        "share_recv": pltpu.VMEM((steps, 2, 8, LANES), F32),
        "rsend": pltpu.VMEM((steps, 2, 2 * cap, half_model), BF16),
        "ret": pltpu.VMEM((nz, 2 * cap, half_model), BF16),
        "ssend": pltpu.VMEM((steps, 2, 8, LANES), F32),
        "sret": pltpu.VMEM((nz, 8, LANES), F32),
        "weights": pltpu.VMEM((2 * rows, nz * 2 * cap), BF16),
        "stage": pltpu.VMEM((nz, tall, LANES), F32),
        "gain_stage": pltpu.VMEM((tall, LANES), F32),
        "q_src": pltpu.VMEM((nz, tall, LANES), BF16),
        "q_dst": pltpu.VMEM((nz, tall, LANES), BF16),
        "x_src": pltpu.VMEM((tall, LANES), F32),
        "x_dst": pltpu.VMEM((tall, LANES), F32),
        "y_src": pltpu.VMEM((tall, LANES), F32),
        "y_dst": pltpu.VMEM((tall, LANES), F32),
        "a_src": pltpu.VMEM((tall, LANES), BF16),
        "a_dst": pltpu.VMEM((nz, tall, LANES), BF16),
        "n_src": pltpu.VMEM((tall, LANES), BF16),
        "n_dst": pltpu.VMEM((nz, tall, LANES), BF16),
        "w_sem": sems(3),
        "l_sem": sems(G_PIECES + X_PIECES + 3),
        "ge_send": sems(2 * G_PIECES),
        "ge_recv": sems(2 * G_PIECES),
        "xe_send": sems(2 * X_PIECES),
        "xe_recv": sems(2 * X_PIECES),
        "gd_send": sems(G_PIECES, steps, 2),
        "gd_recv": sems(G_PIECES, steps, 2),
        "xd_send": sems(X_PIECES, steps, 2),
        "xd_recv": sems(X_PIECES, steps, 2),
        "gf_send": sems(steps, 2),
        "gf_recv": sems(steps, 2),
        "xf_send": sems(steps, 2),
        "xf_recv": sems(steps, 2),
        "p_send": sems(steps),
        "p_recv": sems(steps),
        "h_send": sems(steps),
        "h_recv": sems(steps),
        "r_send": sems(steps, 2),
        "r_recv": sems(steps, 2),
        "s_send": sems(steps, 2),
        "s_recv": sems(steps, 2),
        "q_send": sems(nz),
        "q_recv": sems(nz),
        "x_send": sems(2),
        "x_recv": sems(2),
        "a_send": sems(nz),
        "a_recv": sems(nz),
        "n_send": sems(nz),
        "n_recv": sems(nz),
    }
    operands = ["lengths", "picks", "gain", "router_t", "acts", "cots"]
    operands += ["gate_hbm", "up_hbm", "down_hbm"]
    names = operands + ["lig", "router_total", "gain_total"] + list(scratch)
    return pl.pallas_call(
        functools.partial(kernel, nz, cap, sections, names),
        out_shape=(
            jax.ShapeDtypeStruct((rows, width), BF16),
            jax.ShapeDtypeStruct((nz, width), F32),
            jax.ShapeDtypeStruct((tall, LANES), F32),
        ),
        in_specs=[vmem] * 4 + [anywhere] * 5,
        out_specs=(vmem, vmem, vmem),
        scratch_shapes=list(scratch.values()),
        compiler_params=pltpu.CompilerParams(
            collective_id=0, has_side_effects=True, vmem_limit_bytes=56 * 1024 * 1024
        ),
        cost_estimate=pl.CostEstimate(
            flops=8_000_000_000, bytes_accessed=8_000_000, transcendentals=200_000
        ),
    )(lengths, picks, gain, router_t, acts, cots, gate, up, down)


def per_device(
    activations,
    cotangents,
    norm_gain,
    routes,
    lengths,
    router_weight,
    gate_weight,
    up_weight,
    down_weight,
):
    rows, width = activations.shape[1:]
    experts = router_weight.shape[2]
    top = routes.shape[2]
    cap = 3 * rows * top // (2 * experts)
    lig, router_total, gain_total = exchange(
        experts,
        cap,
        lax.axis_size("section"),
        lengths,
        routes[0].T,
        norm_gain,
        router_weight[0].T,
        activations,
        cotangents,
        gate_weight[0, 0],
        up_weight[0, 0],
        down_weight[0, 0],
    )
    lines = width // LANES
    return (lig[None], router_total.T[None], gain_total[:lines].reshape(1, width))


def solution(mesh):
    in_specs = (
        P("section", "expert", None),
        P("section", "expert", None),
        P("section", None),
        P("section", "expert", None),
        P("section", "expert"),
        P("section", None, None),
        P("section", "expert", None, None),
        P("section", "expert", None, None),
        P("section", "expert", None, None),
    )
    out_specs = (P("section", "expert", None), P("section", None, None), P("section", None))
    return jax.shard_map(
        per_device, mesh=mesh, in_specs=in_specs, out_specs=out_specs, check_vma=False
    )
```

time: 914 us -> 255 us (0.28)
  waiting for transfers between devices: 612 us -> 0 us
  Pallas kernels: 0 us -> 251 us
  local copies, waits for them, and re-layouts: 96.6 us -> 3.21 us
  other arithmetic: 53.5 us -> 0 us
  starting transfers between devices: 50.6 us -> 0 us
  blocking collectives: 48.8 us -> 0 us
  matrix products: 33.5 us -> 0 us
  between operations: 15 us -> 1.3 us
    all_to_all x4 -> x0, waiting for transfers between devices: 459 us -> none  [the longest x2 187 us: deliver(): lax.all_to_all(doubled, 'expert', split_axis=1, concat_axis=1, tiled=True)]
    pallas_call x0 -> x1, Pallas kernels: none -> 251 us  [exchange(): pl.pallas_call(functools.partial(kernel, nz, cap, sections, names), out_s...]
    psum x1 -> x0, waiting for transfers between devices: 129 us -> none  [per_device(): lax.psum(router_term.astype(jnp.bfloat16), 'expert').astype(jnp.float32)]
    unnamed x34 -> x7, local copies, waits for them, and re-layouts: 57 us -> 3.21 us
    psum x1 -> x0, blocking collectives: 48.8 us -> none  [per_device(): lax.psum(gain_contribution.astype(jnp.bfloat16), 'expert')]
    unnamed x2 -> x0, other arithmetic: 41.1 us -> none
    all_to_all x4 -> x0, starting transfers between devices: 40.4 us -> none  [the longest x2 25 us: deliver(): lax.all_to_all(doubled, 'expert', split_axis=1, concat_axis=1, tiled=True)]
    broadcast_in_dim x10 -> x0, local copies, waits for them, and re-layouts: 38.7 us -> none  [the longest x6 38.4 us: deliver(): jnp.broadcast_to(shaped, (stack_count, expert_count, 2, capacity * model_...]
  transfers between devices with their start and end apart: 7 -> 0, of which waited for: 7 -> 0; matrix products, arithmetic and copies ran while one was open for 10% -> 0% of each run, Pallas kernels for 0% -> 0%
where the time goes in v2:
time: 255 us
  Pallas kernels  251 us (98%)
  local copies, waits for them, and re-layouts  3.21 us (1%)
    pallas_call x1, Pallas kernels, exchange(): pl.pallas_call(functools.partial(kernel, nz, cap, sections, names), out_s...  251 us

profile of v2, /device:TPU:1, one launch (start us, length us, event | category | flops | bytes accessed | tf_op | source)
XLA Modules:
  0.0 255.2 jit_solution(10824089320603698348)
XLA Ops:
  1.3 250.7 %shard_map.112 = (bf16[128,2048]{1,0:T(8,128)(2,1)}, f32[16,2048]{1,0:T(8,128)}, f32[16,128]{1,0:T(8,128)}) custom-call(s32[1,1]{1,0:T(1,128)S(6)} %copy.15.refs_0_, s32[2,128]{1,0:T(2,128)} %bitcast.21, bf16[1,2048]{1,0:T(2,128)(2,1)} %refs_2_.1, bf16[16,2048]{1,0:T(8,128)(2,1)} %bitcast.20, bf16[1,128,2048]{2,1,0:T(8,128)(2,1)} %refs_4_.1, ...), custom_call_target="tpu_custom_call" | custom-call | flops 8000000000 | bytes 8000000 | tf_op jit(solution)/shard_map/pallas_call | solution.py:611
  252.0 0.0 copy-start
  252.0 1.9 copy.16
  254.0 0.0 copy-done
  254.0 0.0 copy-start.1
  254.0 0.7 copy.17
  254.6 0.0 copy-done.1
  254.7 0.6 copy.18
Async XLA Ops:
  252.0 1.9 copy-start
  254.0 0.7 copy-start.1

commit v3 on v2

--- a/solution.py
+++ b/solution.py
@@ -41,6 +41,7 @@
     g_wide = half_model // G_PIECES
     x_wide = half_model // X_PIECES
     blocks = width // LANES
+    r_first, r_second = steps // 2, 3 * steps // 4
     section = lax.axis_index("section")
     me = lax.axis_index("expert")
     chip = me // 2
@@ -145,6 +146,16 @@
             r.ssend.at[step, side], r.sret.at[chip], (r.s_send, r.s_recv), (step, side), target
         )
 
+    def give_gates(step, side):
+        target = at_offset(offset_of(step, side))
+        return remote(
+            r.gate_out.at[target // 2],
+            r.gate_in.at[step, side],
+            (r.gg_send, r.gg_recv),
+            (step, side),
+            target,
+        )
+
     def reduce_router(offset):
         target = at_offset(offset)
         return remote(
@@ -156,12 +167,7 @@
             r.a_src, r.a_dst.at[chip], (r.a_send, r.a_recv), offset, at_offset(offset)
         )
 
-    def gather_gain(offset):
-        return remote(
-            r.n_src, r.n_dst.at[offset], (r.n_send, r.n_recv), offset, at_offset(offset)
-        )
-
-    def pairs(body):
+    def pairs(body, first=0, last=steps):
         def both(step, carry):
             body(step, 0)
 
@@ -171,7 +177,7 @@
 
             return carry
 
-        lax.fori_loop(0, steps, both, 0)
+        lax.fori_loop(first, last, both, 0)
 
     def others(body):
         def one(offset, carry):
@@ -180,6 +186,16 @@
 
         lax.fori_loop(1, nz, one, 0)
 
+    barrier = pltpu.get_barrier_semaphore()
+
+    def greet(offset):
+        pl.semaphore_signal(
+            barrier, inc=1, device_id=(section, at_offset(offset)), device_id_type=MESH
+        )
+
+    others(greet)
+    for home, target in ((section, sibling), (section_before, me), (section_after, me)):
+        pl.semaphore_signal(barrier, inc=1, device_id=(home, target), device_id_type=MESH)
     loads = [
         pltpu.make_async_copy(r.gate_hbm, r.gate_w, r.w_sem.at[0]),
         pltpu.make_async_copy(r.up_hbm, r.up_w, r.w_sem.at[1]),
@@ -203,16 +219,6 @@
         chosen = (slots == targets[0] + part * cap) | (slots == targets[1] + part * cap)
         r.select[:, part * rows : (part + 1) * rows] = jnp.where(chosen, 1.0, 0.0).astype(BF16)
 
-    barrier = pltpu.get_barrier_semaphore()
-
-    def greet(offset):
-        pl.semaphore_signal(
-            barrier, inc=1, device_id=(section, at_offset(offset)), device_id_type=MESH
-        )
-
-    others(greet)
-    for home, target in ((section, sibling), (section_before, me), (section_after, me)):
-        pl.semaphore_signal(barrier, inc=1, device_id=(home, target), device_id_type=MESH)
     pl.semaphore_wait(barrier, nz + 2)
 
     for piece in range(G_PIECES):
@@ -281,6 +287,17 @@
         for k in range(2)
     ]
     gates = [1.0 / (1.0 + jnp.exp(scores[1 - k] - scores[k])) for k in range(2)]
+    places = iota((rows, LANES), 1)
+    place_of = [target_of[k] - picked[k] * (2 * cap) for k in range(2)]
+    slot_gates = jnp.zeros((nz, LANES), F32)
+    for k in range(2):
+        onehot = jnp.where(named[k], 1.0, 0.0).astype(BF16)
+        for piece in split(jnp.where(places == place_of[k], gates[k], 0.0)):
+            slot_gates = slot_gates + dot(onehot, piece)
+    r.gate_out[...] = slot_gates.reshape(nz, 1, LANES)
+    pairs(lambda step, side: give_gates(step, side).start())
+    r.gate_in[0, 1] = r.gate_out[chip]
+    r.gain_sum[...] = jnp.zeros_like(r.gain_sum)
     across_slots = iota((rows, nz * 2 * cap), 1)
     for part in range(2):
         mix = jnp.where(across_slots == target_of[0] + part * cap, gates[0], 0.0)
@@ -354,11 +371,10 @@
         for which in range(4):
             column = share[which * cap : (which + 1) * cap]
             line = jnp.sum(jnp.where(diagonal, column, 0.0), axis=0, keepdims=True)
-            tile = jnp.broadcast_to(line, (8, LANES))
             if which < 2:
-                r.own_share[step, which] = tile
+                r.own_share[step, which] = line
             else:
-                r.share_send[step, which - 2] = tile
+                r.share_send[step, which - 2] = line
         partial_share(step).start()
         gate_grad = (
             hidden_grad * up_pre * logistic * (1.0 + gate_pre * (1.0 - logistic))
@@ -386,15 +402,33 @@
 
         partial(step).wait_recv()
         total = r.own[step] + r.precv[step].astype(F32)
+        stacked = []
         for side in range(2):
             mine = total[side * cap : (side + 1) * cap]
-            stacked = jnp.concatenate([mine[:, :half_model], mine[:, half_model:]], axis=0)
-            r.rsend[step, side] = stacked.astype(BF16)
-        give_back(step, 0).start()
+            stacked.append(jnp.concatenate([mine[:, :half_model], mine[:, half_model:]], axis=0))
+            r.rsend[step, side] = stacked[side].astype(BF16)
+        @pl.when(step < r_first)
+        def _():
+            give_back(step, 0).start()
+
+        @pl.when((step > 0) & (step < r_first))
+        def _():
+            give_back(step, 1).start()
+
+        give_gates(step, 0).wait_recv()
 
         @pl.when(step > 0)
         def _():
-            give_back(step, 1).start()
+            give_gates(step, 1).wait_recv()
+
+        for side in range(2):
+            line = r.gate_in[step, side]
+            column = jnp.sum(jnp.where(diagonal, line, 0.0), axis=1, keepdims=True)
+            term = stacked[side] * r.xbuf[step, side, 0].astype(F32)
+            for part in range(2):
+                r.gain_sum[part : part + 1, :] += jnp.sum(
+                    term[part * cap : (part + 1) * cap] * column, axis=0, keepdims=True
+                )
 
     def pipeline_g(turn, carry):
         @pl.when(turn < steps)
@@ -430,19 +464,24 @@
     self_share = pltpu.make_async_copy(r.ssend.at[0, 1], r.sret.at[chip], r.l_sem.at[base + 1])
     self_back.start()
     self_share.start()
+    for block in range(blocks):
+        part, column = divmod(block * LANES, half_model)
+        r.y_src[block : block + 1, :] = r.gain_sum[part : part + 1, column : column + LANES]
+    across_gain = remote(r.y_src, r.y_dst, (r.x_send, r.x_recv), 1, sibling)
+    across_gain.start()
     self_share.wait()
     pairs(lambda step, side: give_share(step, side).wait_recv())
 
-    shares = jnp.max(r.sret[...], axis=1)
-    places = iota((rows, LANES), 1)
+    shares = r.sret[...].reshape(nz, LANES)
     first, second = split(shares)
     third = (shares - first.astype(F32) - second.astype(F32)).astype(BF16)
     gate_share = []
     for k in range(2):
         onehot = jnp.where(expert_ids == picked[k], 1.0, 0.0).astype(BF16)
         line = dot(onehot, first) + dot(onehot, second) + dot(onehot, third)
-        place = target_of[k] - picked[k] * (2 * cap)
-        gate_share.append(jnp.sum(jnp.where(places == place, line, 0.0), axis=1, keepdims=True))
+        gate_share.append(
+            jnp.sum(jnp.where(places == place_of[k], line, 0.0), axis=1, keepdims=True)
+        )
     mean_share = gates[0] * gate_share[0] + gates[1] * gate_share[1]
     logit_grad = jnp.zeros((rows, nz), F32)
     for k in range(2):
@@ -454,43 +493,42 @@
         r.stage[:, block, :] = router_term[:, block * LANES : (block + 1) * LANES]
     r.q_src[...] = r.stage[...].astype(BF16)
     others(lambda offset: reduce_router(offset).start())
+    pairs(lambda step, side: give_back(step, side).start(), r_first, r_second)
     self_reduce = pltpu.make_async_copy(r.q_src.at[chip], r.q_dst.at[0], r.l_sem.at[base + 2])
     self_reduce.start()
     router_part = dot(grad_high, r.router_t[...]) + dot(grad_low, r.router_t[...])
 
+    self_reduce.wait()
+    others(lambda offset: reduce_router(offset).wait_recv())
+    r.x_src[...] = jnp.sum(r.q_dst[...].astype(F32), axis=0)
+    across_router = remote(r.x_src, r.x_dst, (r.x_send, r.x_recv), 0, sibling)
+    across_router.start()
+
+    across_gain.wait_recv()
+    across_router.wait_recv()
+    router_row = r.x_src[...] + r.x_dst[...]
+    gain_row = r.y_src[...] + r.y_dst[...]
+    mine = lax.rem(chip, 2) == core
+    r.a_src[...] = jnp.where(mine, router_row, gain_row).astype(BF16)
+    others(lambda offset: gather_router(offset).start())
+    r.a_dst[chip] = r.a_src[...]
+
+    pairs(lambda step, side: give_back(step, side).start(), r_second, steps)
     self_back.wait()
     pairs(lambda step, side: give_back(step, side).wait_recv())
     came_back = r.ret[...].reshape(nz * 2 * cap, half_model)
     both = dot(r.weights[...], came_back)
     normed_grad = jnp.concatenate([both[:rows], both[rows:]], axis=1) + router_part
+
     unit = sides(r.xex, X_PIECES).astype(F32) * inv
-    gain_term = jnp.sum(normed_grad * unit, axis=0, keepdims=True)
-    for block in range(blocks):
-        r.gain_stage[block : block + 1, :] = gain_term[:, block * LANES : (block + 1) * LANES]
-    r.n_src[...] = r.gain_stage[...].astype(BF16)
-    others(lambda offset: gather_gain(offset).start())
-    r.n_dst[0] = r.n_src[...]
-
-    self_reduce.wait()
-    others(lambda offset: reduce_router(offset).wait_recv())
-    r.x_src[...] = jnp.sum(r.q_dst[...].astype(F32), axis=0)
-    across_router = remote(r.x_src, r.x_dst, (r.x_send, r.x_recv), 0, sibling)
-    across_router.start()
-
     scaled = normed_grad * r.gain[...].astype(F32)
     mean_scaled = jnp.mean(scaled * unit, axis=-1, keepdims=True)
     returned = sides(r.gex, G_PIECES).astype(F32)
     r.lig[...] = (returned + inv * (scaled - unit * mean_scaled)).astype(BF16)
 
-    across_router.wait_recv()
-    r.a_src[...] = (r.x_src[...] + r.x_dst[...]).astype(BF16)
-    others(lambda offset: gather_router(offset).start())
-    r.a_dst[chip] = r.a_src[...]
-
-    others(lambda offset: gather_gain(offset).wait_recv())
-    r.y_src[...] = jnp.sum(r.n_dst[...].astype(F32), axis=0)
-    across_gain = remote(r.y_src, r.y_dst, (r.x_send, r.x_recv), 1, sibling)
-    across_gain.start()
+    others(lambda offset: gather_router(offset).wait_recv())
+    swap = remote(r.a_dst, r.b_dst, (r.x_send, r.x_recv), 2, sibling)
+    swap.start()
 
     for piece in range(G_PIECES):
         for part in range(2):
@@ -513,14 +551,26 @@
     pairs(lambda step, side: give_back(step, side).wait_send())
     pairs(lambda step, side: give_share(step, side).wait_send())
     others(lambda offset: reduce_router(offset).wait_send())
-    others(lambda offset: gather_gain(offset).wait_send())
-
+    others(lambda offset: gather_router(offset).wait_send())
+    pairs(lambda step, side: give_gates(step, side).wait_send())
     across_router.wait_send()
-    across_gain.wait()
-    r.gain_total[...] = r.y_src[...] + r.y_dst[...]
-    others(lambda offset: gather_router(offset).wait())
+    across_gain.wait_send()
+
+    swap.wait()
+    here = r.a_dst[...].astype(F32)
+    there = r.b_dst[...].astype(F32)
+    tall = here.shape[1]
+    is_here = lax.rem(iota((nz, tall, LANES), 0), 2) == core
+    router_rows = jnp.where(is_here, here, there)
+    gain_rows = jnp.sum(jnp.where(is_here, there, here), axis=0)
     for block in range(blocks):
-        r.router_total[:, block * LANES : (block + 1) * LANES] = r.a_dst[:, block, :].astype(F32)
+        columns = slice(block * LANES, (block + 1) * LANES)
+        total = router_rows[:, block, :]
+        r.router_total[:, columns] = total
+        from_router = jnp.sum(total * r.router_t[:, columns].astype(F32), axis=0, keepdims=True)
+        r.gain_total[:, columns] = (gain_rows[block : block + 1, :] + from_router) / r.gain[
+            :, columns
+        ].astype(F32)
 
 
 def exchange(nz, cap, sections, lengths, picks, gain, router_t, acts, cots, gate, up, down):
@@ -554,16 +604,18 @@
         "own": pltpu.VMEM((steps, 2 * cap, width), F32),
         "psend": pltpu.VMEM((steps, 2 * cap, width), BF16),
         "precv": pltpu.VMEM((steps, 2 * cap, width), BF16),
-        "own_share": pltpu.VMEM((steps, 2, 8, LANES), F32),
-        "share_send": pltpu.VMEM((steps, 2, 8, LANES), F32),
-        "share_recv": pltpu.VMEM((steps, 2, 8, LANES), F32),
+        "own_share": pltpu.VMEM((steps, 2, 1, LANES), F32),
+        "share_send": pltpu.VMEM((steps, 2, 1, LANES), F32),
+        "share_recv": pltpu.VMEM((steps, 2, 1, LANES), F32),
         "rsend": pltpu.VMEM((steps, 2, 2 * cap, half_model), BF16),
         "ret": pltpu.VMEM((nz, 2 * cap, half_model), BF16),
-        "ssend": pltpu.VMEM((steps, 2, 8, LANES), F32),
-        "sret": pltpu.VMEM((nz, 8, LANES), F32),
+        "ssend": pltpu.VMEM((steps, 2, 1, LANES), F32),
+        "sret": pltpu.VMEM((nz, 1, LANES), F32),
+        "gate_out": pltpu.VMEM((nz, 1, LANES), F32),
+        "gate_in": pltpu.VMEM((steps, 2, 1, LANES), F32),
+        "gain_sum": pltpu.VMEM((2, half_model), F32),
         "weights": pltpu.VMEM((2 * rows, nz * 2 * cap), BF16),
         "stage": pltpu.VMEM((nz, tall, LANES), F32),
-        "gain_stage": pltpu.VMEM((tall, LANES), F32),
         "q_src": pltpu.VMEM((nz, tall, LANES), BF16),
         "q_dst": pltpu.VMEM((nz, tall, LANES), BF16),
         "x_src": pltpu.VMEM((tall, LANES), F32),
@@ -572,8 +624,7 @@
         "y_dst": pltpu.VMEM((tall, LANES), F32),
         "a_src": pltpu.VMEM((tall, LANES), BF16),
         "a_dst": pltpu.VMEM((nz, tall, LANES), BF16),
-        "n_src": pltpu.VMEM((tall, LANES), BF16),
-        "n_dst": pltpu.VMEM((nz, tall, LANES), BF16),
+        "b_dst": pltpu.VMEM((nz, tall, LANES), BF16),
         "w_sem": sems(3),
         "l_sem": sems(G_PIECES + X_PIECES + 3),
         "ge_send": sems(2 * G_PIECES),
@@ -598,12 +649,12 @@
         "s_recv": sems(steps, 2),
         "q_send": sems(nz),
         "q_recv": sems(nz),
-        "x_send": sems(2),
-        "x_recv": sems(2),
+        "x_send": sems(3),
+        "x_recv": sems(3),
+        "gg_send": sems(steps, 2),
+        "gg_recv": sems(steps, 2),
         "a_send": sems(nz),
         "a_recv": sems(nz),
-        "n_send": sems(nz),
-        "n_recv": sems(nz),
     }
     operands = ["lengths", "picks", "gain", "router_t", "acts", "cots"]
     operands += ["gate_hbm", "up_hbm", "down_hbm"]
@@ -613,13 +664,13 @@
         out_shape=(
             jax.ShapeDtypeStruct((rows, width), BF16),
             jax.ShapeDtypeStruct((nz, width), F32),
-            jax.ShapeDtypeStruct((tall, LANES), F32),
+            jax.ShapeDtypeStruct((1, width), F32),
         ),
         in_specs=[vmem] * 4 + [anywhere] * 5,
         out_specs=(vmem, vmem, vmem),
         scratch_shapes=list(scratch.values()),
         compiler_params=pltpu.CompilerParams(
-            collective_id=0, has_side_effects=True, vmem_limit_bytes=56 * 1024 * 1024
+            collective_id=0, has_side_effects=True, vmem_limit_bytes=44 * 1024 * 1024
         ),
         cost_estimate=pl.CostEstimate(
             flops=8_000_000_000, bytes_accessed=8_000_000, transcendentals=200_000
@@ -656,8 +707,7 @@
         up_weight[0, 0],
         down_weight[0, 0],
     )
-    lines = width // LANES
-    return (lig[None], router_total.T[None], gain_total[:lines].reshape(1, width))
+    return (lig[None], router_total.T[None], gain_total)
 
 
 def solution(mesh):

time: 255 us -> 251 us (0.984)
  Pallas kernels: 251 us -> 240 us
  local copies, waits for them, and re-layouts: 3.21 us -> 9.32 us
    pallas_call x1, Pallas kernels: 251 us -> 240 us  [exchange(): pl.pallas_call(functools.partial(kernel, nz, cap, sections, names), out_s...]
    unnamed x7 -> x19, local copies, waits for them, and re-layouts: 3.21 us -> 9.32 us
where the time goes in v3:
time: 251 us
  Pallas kernels  240 us (96%)
  local copies, waits for them, and re-layouts  9.32 us (4%)
    pallas_call x1, Pallas kernels, exchange(): pl.pallas_call(functools.partial(kernel, nz, cap, sections, names), out_s...  240 us
    unnamed x19, local copies, waits for them, and re-layouts  9.32 us

profile of v3, /device:TPU:1, one launch (start us, length us, event | category | flops | bytes accessed | tf_op | source)
XLA Modules:
  0.0 250.7 jit_solution(15993664174883054823)
XLA Ops:
  0.6 0.0 copy-start.6
  1.3 0.0 copy-start.7
  1.3 0.0 copy-done.6
  1.3 0.7 copy-done.7
  2.0 0.0 copy-start
  2.0 1.2 copy-done
  3.2 0.0 copy-start.1
  3.2 1.2 copy-done.1
  4.4 0.0 copy-start.2
  4.4 1.2 copy-done.2
  5.7 0.0 copy-start.3
  5.7 1.0 copy-done.3
  6.7 0.0 copy-start.4
  6.7 1.0 copy-done.4
  7.7 0.0 copy-start.5
  7.7 0.8 copy-done.5
  8.6 240.1 %shard_map.112 = (bf16[128,2048]{1,0:T(8,128)(2,1)S(1)}, f32[16,2048]{1,0:T(8,128)S(1)}, f32[1,2048]{1,0:T(1,128)S(1)}) custom-call(s32[1,1]{1,0:T(1,128)S(6)} %copy.15.refs_0_, s32[2,128]{1,0:T(2,128)S(1)} %bitcast.19, bf16[1,2048]{1,0:T(2,128)(2,1)S(1)} %copy-done.6, bf16[16,2048]{1,0:T(8,128)(2,1)S(1)} %bitcast.18, bf16[1,128,2048]{2,1,0:T(8,128)(2,1)S(1)} %copy-done.3, ...), custom_call_target="tpu_custom_call" | custom-call | flops 8000000000 | bytes 8000000 | tf_op jit(solution)/shard_map/pallas_call | solution.py:662
  248.7 0.8 copy.16
  249.5 0.7 copy.17
  250.1 0.6 copy.18
Async XLA Ops:
  0.6 0.7 copy-start.6
  1.3 0.7 copy-start.7
  2.0 1.2 copy-start
  3.2 1.2 copy-start.1
  4.4 1.2 copy-start.2
  5.7 1.0 copy-start.3
  6.7 1.0 copy-start.4
  7.7 0.8 copy-start.5

commit v4 on v3

--- a/solution.py
+++ b/solution.py
@@ -12,6 +12,7 @@
 LANES = 128
 G_PIECES = 4
 X_PIECES = 1
+X_FIRST = 4
 MESH = pl.DeviceIdType.MESH
 F32 = jnp.float32
 BF16 = jnp.bfloat16
@@ -42,6 +43,7 @@
     x_wide = half_model // X_PIECES
     blocks = width // LANES
     r_first, r_second = steps // 2, 3 * steps // 4
+    x_first = min(X_FIRST, steps)
     section = lax.axis_index("section")
     me = lax.axis_index("expert")
     chip = me // 2
@@ -265,7 +267,9 @@
         )
         spread = dot(r.select[...], both).astype(BF16)
         r.dispx[piece] = spread.reshape(nz, 2 * cap, x_wide)
-        pairs(lambda step, side, piece=piece: dispatch_x(piece, step, side).start())
+        pairs(
+            lambda step, side, piece=piece: dispatch_x(piece, step, side).start(), 0, x_first
+        )
         own_copies.append(
             pltpu.make_async_copy(
                 r.dispx.at[piece, chip], r.xbuf.at[0, 1, piece], r.l_sem.at[len(own_copies)]
@@ -445,6 +449,12 @@
         @pl.when(turn < steps)
         def _():
             receive_x(turn)
+
+        @pl.when(turn < steps - x_first)
+        def _():
+            for piece in range(X_PIECES):
+                for side in range(2):
+                    dispatch_x(piece, turn + x_first, side).start()
 
         @pl.when((turn >= 1) & (turn <= steps))
         def _():

time: 251 us -> 250 us (level)
  no operation moved by 1% of the time
where the time goes in v4:
time: 250 us; the launch traced here: 249 us
  Pallas kernels  239 us (96%)
  local copies, waits for them, and re-layouts  9.32 us (4%)
    pallas_call x1, Pallas kernels, exchange(): pl.pallas_call(functools.partial(kernel, nz, cap, sections, names), out_s...  239 us
    unnamed x19, local copies, waits for them, and re-layouts  9.32 us

profile of v4, /device:TPU:1, one launch (start us, length us, event | category | flops | bytes accessed | tf_op | source)
XLA Modules:
  0.0 249.3 jit_solution(13313443285078429768)
XLA Ops:
  0.6 0.0 copy-start.6
  1.3 0.0 copy-start.7
  1.3 0.0 copy-done.6
  1.3 0.7 copy-done.7
  2.0 0.0 copy-start
  2.0 1.2 copy-done
  3.2 0.0 copy-start.1
  3.2 1.2 copy-done.1
  4.4 0.0 copy-start.2
  4.4 1.2 copy-done.2
  5.7 0.0 copy-start.3
  5.7 1.0 copy-done.3
  6.7 0.0 copy-start.4
  6.7 1.0 copy-done.4
  7.7 0.0 copy-start.5
  7.7 0.8 copy-done.5
  8.6 238.7 %shard_map.112 = (bf16[128,2048]{1,0:T(8,128)(2,1)S(1)}, f32[16,2048]{1,0:T(8,128)S(1)}, f32[1,2048]{1,0:T(1,128)S(1)}) custom-call(s32[1,1]{1,0:T(1,128)S(6)} %copy.15.refs_0_, s32[2,128]{1,0:T(2,128)S(1)} %bitcast.19, bf16[1,2048]{1,0:T(2,128)(2,1)S(1)} %copy-done.6, bf16[16,2048]{1,0:T(8,128)(2,1)S(1)} %bitcast.18, bf16[1,128,2048]{2,1,0:T(8,128)(2,1)S(1)} %copy-done.3, ...), custom_call_target="tpu_custom_call" | custom-call | flops 8000000000 | bytes 8000000 | tf_op jit(solution)/shard_map/pallas_call | solution.py:672
  247.3 0.8 copy.16
  248.1 0.7 copy.17
  248.7 0.6 copy.18
Async XLA Ops:
  0.6 0.7 copy-start.6
  1.3 0.7 copy-start.7
  2.0 1.2 copy-start
  3.2 1.2 copy-start.1
  4.4 1.2 copy-start.2
  5.7 1.0 copy-start.3
  6.7 1.0 copy-start.4
  7.7 0.8 copy-start.5

commit v5 on v4

--- a/solution.py
+++ b/solution.py
@@ -223,17 +223,15 @@
 
     pl.semaphore_wait(barrier, nz + 2)
 
-    for piece in range(G_PIECES):
-        for part in range(2):
-            hand_back(part, piece).start()
-    for piece in range(X_PIECES):
-        for part in range(2):
-            hand_on(part, piece).start()
-
+    for part in range(2):
+        hand_back(part, 0).start()
     own_copies = []
     for piece in range(G_PIECES):
         for part in range(2):
             hand_back(part, piece).wait_recv()
+        if piece + 1 < G_PIECES:
+            for part in range(2):
+                hand_back(part, piece + 1).start()
         spread = dot(r.select[...], r.gex[piece]).astype(BF16)
         r.dispg[piece] = spread.reshape(nz, 2 * cap, g_wide)
         pairs(lambda step, side, piece=piece: dispatch_g(piece, step, side).start())
@@ -243,6 +241,10 @@
             )
         )
         own_copies[-1].start()
+        if piece == G_PIECES // 2 - 1:
+            for x_piece in range(X_PIECES):
+                for part in range(2):
+                    hand_on(part, x_piece).start()
 
     for piece in range(X_PIECES):
         for part in range(2):

time: 250 us -> 250 us (level)
  no operation moved by 1% of the time
where the time goes in v5:
time: 250 us; the launch traced here: 249 us
  Pallas kernels  239 us (96%)
  local copies, waits for them, and re-layouts  9.32 us (4%)
    pallas_call x1, Pallas kernels, exchange(): pl.pallas_call(functools.partial(kernel, nz, cap, sections, names), out_s...  239 us
    unnamed x19, local copies, waits for them, and re-layouts  9.32 us

profile of v5, /device:TPU:1, one launch (start us, length us, event | category | flops | bytes accessed | tf_op | source)
XLA Modules:
  0.0 249.2 jit_solution(2365726403606884359)
XLA Ops:
  0.6 0.0 copy-start.6
  1.3 0.0 copy-start.7
  1.3 0.0 copy-done.6
  1.3 0.7 copy-done.7
  2.0 0.0 copy-start
  2.0 1.2 copy-done
  3.2 0.0 copy-start.1
  3.2 1.2 copy-done.1
  4.4 0.0 copy-start.2
  4.4 1.2 copy-done.2
  5.7 0.0 copy-start.3
  5.7 1.0 copy-done.3
  6.7 0.0 copy-start.4
  6.7 1.0 copy-done.4
  7.7 0.0 copy-start.5
  7.7 0.8 copy-done.5
  8.6 238.6 %shard_map.112 = (bf16[128,2048]{1,0:T(8,128)(2,1)S(1)}, f32[16,2048]{1,0:T(8,128)S(1)}, f32[1,2048]{1,0:T(1,128)S(1)}) custom-call(s32[1,1]{1,0:T(1,128)S(6)} %copy.15.refs_0_, s32[2,128]{1,0:T(2,128)S(1)} %bitcast.19, bf16[1,2048]{1,0:T(2,128)(2,1)S(1)} %copy-done.6, bf16[16,2048]{1,0:T(8,128)(2,1)S(1)} %bitcast.18, bf16[1,128,2048]{2,1,0:T(8,128)(2,1)S(1)} %copy-done.3, ...), custom_call_target="tpu_custom_call" | custom-call | flops 8000000000 | bytes 8000000 | tf_op jit(solution)/shard_map/pallas_call | solution.py:674
  247.2 0.8 copy.16
  248.0 0.7 copy.17
  248.6 0.6 copy.18
Async XLA Ops:
  0.6 0.7 copy-start.6
  1.3 0.7 copy-start.7
  2.0 1.2 copy-start
  3.2 1.2 copy-start.1
  4.4 1.2 copy-start.2
  5.7 1.0 copy-start.3
  6.7 1.0 copy-start.4
  7.7 0.8 copy-start.5
